TPU v7x, 128 devices: a whole 4x4x4 slice. The times are simulated.
128 devices in a mesh: nest: 2 (over y_hi), gx: 64 (over y_lo, x, z, core).
Axes of the slice: x: 4, y: 4 (y_hi: 2, y_lo: 2; y = y_hi * 2 + y_lo), z: 4, core: 2. Of those that a mesh axis runs over, the one named last changes fastest.
Arguments:
- velocity: float32 [2, 3, 8, 1024, 2048], P('nest', None, None, 'gx'), may hold values from -6 to 6
- viscosity: float32 [2, 8, 1024, 2048], P('nest', None, 'gx'), may hold values from 0.02 to 0.5
- heights: int32 [2, 1024, 2048], P('nest', 'gx'), may hold values from 0 to 4
- row_offset: int32 [1], replicated, may hold values from 0 to 512
- column_offset: int32 [1], replicated, may hold values from 0 to 2047
Outputs:
- new_velocity: float32 [2, 3, 8, 1024, 2048], P('nest', None, None, 'gx')
- pressure: float32 [2, 8, 1024, 2048], P('nest', None, 'gx')
All inputs are finite; a program needn't handle non-finite values.
Results may differ from a plain program's by a relative error of at most 0.00012.
Values sent between devices are 32-bit elements; how exact they have to be, the bound alone decides.
A program may use at most 192 MiB of HBM per device.

v0:
```python
import math

import jax
import jax.numpy as jnp
from jax import lax
from jax.sharding import PartitionSpec as P

time_step = 0.2
blend_rate = 0.5
highest = lax.Precision.HIGHEST


def with_halo(cells, sides, width):
    for axis, dim in sides:
        count = lax.axis_size(axis)
        head = lax.slice_in_dim(cells, 0, width, axis=dim)
        tail = lax.slice_in_dim(cells, cells.shape[dim] - width, cells.shape[dim], axis=dim)
        cells = jnp.concatenate(
            [
                lax.ppermute(tail, axis, [(i, (i + 1) % count) for i in range(count)]),
                cells,
                lax.ppermute(head, axis, [((i + 1) % count, i) for i in range(count)]),
            ],
            axis=dim,
        )
    return cells


def swapped(value, axis, stride):
    mask = 2**stride
    pairs = [(source, source ^ mask) for source in range(lax.axis_size(axis))]
    return lax.ppermute(value, axis, pairs)


def from_behind(value, axis, steps):
    count = lax.axis_size(axis)
    pairs = [(source, (source + steps) % count) for source in range(count)]
    return lax.ppermute(value, axis, pairs)


def open_cells(roof_level, levels):
    level_index = jnp.arange(levels, dtype=jnp.int32)[:, None, None]
    return (level_index >= roof_level[None]).astype(jnp.float32)


def advance(flow_ext, kappa_ext):
    flow = flow_ext[:, :, 1:-1]
    kappa = kappa_ext[:, 1:-1]
    east_cells = flow_ext[:, :, 2:]
    west_cells = flow_ext[:, :, :-2]
    north_cells = jnp.roll(flow, -1, axis=3)
    south_cells = jnp.roll(flow, 1, axis=3)
    blank = jnp.zeros_like(flow[:, :1])
    upper_cells = jnp.concatenate([flow[:, 1:], blank], axis=1)
    lower_cells = jnp.concatenate([blank, flow[:, :-1]], axis=1)
    face_east = 0.5 * (kappa + kappa_ext[:, 2:])
    face_west = 0.5 * (kappa + kappa_ext[:, :-2])
    face_north = 0.5 * (kappa + jnp.roll(kappa, -1, axis=2))
    face_south = 0.5 * (kappa + jnp.roll(kappa, 1, axis=2))
    face_top = 0.5 * (kappa + jnp.concatenate([kappa[1:], kappa[-1:]], axis=0))
    face_bottom = 0.5 * (kappa + jnp.concatenate([kappa[:1], kappa[:-1]], axis=0))
    carried = 0.5 * (
        flow[0] * (east_cells - west_cells)
        + flow[1] * (north_cells - south_cells)
        + flow[2] * (upper_cells - lower_cells)
    )
    spread = face_east * (east_cells - flow) - face_west * (flow - west_cells)
    spread = spread + face_north * (north_cells - flow) - face_south * (flow - south_cells)
    spread = spread + face_top * (upper_cells - flow) - face_bottom * (flow - lower_cells)
    return flow + time_step * (spread - carried)


def thomas(levels, eigen):
    count = len(levels)
    pivots = []
    partials = []
    for level in range(count):
        diagonal = -1.0 - eigen if level == 0 else -2.0 - eigen
        if level == 0:
            pivot = diagonal
            scaled = levels[0] / pivot
        else:
            pivot = diagonal - 1.0 / pivots[-1]
            scaled = (levels[level] - partials[-1]) / pivot
        pivots.append(pivot)
        partials.append(scaled)
    result = [None] * count
    result[count - 1] = partials[count - 1]
    for level in range(count - 2, -1, -1):
        result[level] = partials[level] - result[level + 1] / pivots[level]
    return result


def hartley_table(count):
    indices = jnp.arange(count, dtype=jnp.int32)
    product = indices[:, None] * indices[None, :] % count
    angle = product.astype(jnp.float32) * (2.0 * math.pi / count)
    return jnp.cos(angle) + jnp.sin(angle)


def local(velocity, viscosity, heights, row_offset, column_offset):
    fields = velocity[0]
    viscous = viscosity[0]
    roof_level = heights[0]
    levels = fields.shape[1]
    row_count = fields.shape[2]
    columns = fields.shape[3]
    group_size = lax.axis_size("gx")
    x_total = row_count * group_size
    y_slab = columns // group_size
    half_y = columns // 2
    half_slab = half_y // group_size
    fluid_mask = open_cells(roof_level, levels)
    row_start = row_offset[0]
    column_start = column_offset[0]
    stacked = jnp.concatenate([fields, viscous[None]], axis=0)
    padded = with_halo(stacked, (("gx", 2),), 1)
    provisional = advance(padded[:3], padded[3]) * fluid_mask
    is_child = lax.axis_index("nest") == 1
    y_index = jnp.arange(columns, dtype=jnp.int32)
    j_index = jnp.arange(half_y, dtype=jnp.int32)
    pair_table = 0.5 * (y_index[:, None] // 2 == j_index[None, :]).astype(jnp.float32)
    select_table = ((column_start + j_index[None, :]) % columns == y_index[:, None]).astype(
        jnp.float32
    )
    outward_table = jnp.where(is_child, pair_table, select_table)
    outgoing = jnp.einsum("czxy,yj->cxzj", provisional, outward_table, precision=highest)
    column_view = lax.all_to_all(outgoing, "gx", split_axis=3, concat_axis=1, tiled=True)
    rows = lax.dynamic_slice_in_dim(column_view, row_start, x_total // 2, axis=1)
    following = jnp.concatenate([rows[:, 1:], rows[:, -1:]], axis=1)
    odd_rows = 0.5 * (rows + following)
    widened = jnp.stack([rows, odd_rows], axis=2).reshape(3, x_total, levels, half_slab)
    paired = column_view.reshape(3, x_total // 2, 2, levels, half_slab)
    averaged = 0.5 * (paired[:, :, 0] + paired[:, :, 1])
    placed = lax.dynamic_update_slice_in_dim(
        jnp.zeros_like(column_view), averaged, row_start, axis=1
    )
    sending = jnp.where(is_child, placed, widened)
    received = swapped(sending, "nest", 0)
    incoming = lax.all_to_all(received, "gx", split_axis=1, concat_axis=3, tiled=True)
    half_of_y = y_index // 2
    upper_pick = jnp.minimum(half_of_y + 1, half_y - 1)
    is_even = y_index % 2 == 0
    own_pick = (half_of_y[None, :] == j_index[:, None]).astype(jnp.float32)
    next_pick = (upper_pick[None, :] == j_index[:, None]).astype(jnp.float32)
    widen_table = jnp.where(is_even[None, :], own_pick, 0.5 * (own_pick + next_pick))
    local_j = (y_index - column_start) % columns
    place_table = (local_j[None, :] == j_index[:, None]).astype(jnp.float32)
    inward_table = jnp.where(is_child, widen_table, place_table)
    mapped = jnp.einsum("cxzj,jy->czxy", incoming, inward_table, precision=highest)
    first_row = lax.axis_index("gx") * row_count
    global_rows = first_row + jnp.arange(row_count, dtype=jnp.int32)
    distance_y = jnp.minimum(y_index, columns - 1 - y_index)
    distance_x = jnp.minimum(global_rows, x_total - 1 - global_rows)
    distance = jnp.minimum(distance_x[:, None], distance_y[None, :]).astype(jnp.float32)
    relax_rate = 0.2 + 0.8 * jnp.exp(-distance * (16.0 / columns))
    child_value = provisional + relax_rate * (mapped - provisional)
    inside_rows = (global_rows >= row_start) & (global_rows < row_start + x_total // 2)
    inside = inside_rows[:, None] & (local_j < half_y)[None, :]
    parent_value = provisional + blend_rate * jnp.where(
        inside[None, None], mapped - provisional, 0.0
    )
    coupled = jnp.where(is_child, child_value, parent_value) * fluid_mask
    table_y = hartley_table(columns)
    table_x = hartley_table(x_total)
    flow_x, flow_y, flow_z = (coupled[0], coupled[1], coupled[2])
    diff_y = flow_y - jnp.roll(flow_y, 1, axis=2)
    diff_z = flow_z - jnp.concatenate([jnp.zeros_like(flow_z[:1]), flow_z[:-1]], axis=0)
    west_row = from_behind(flow_x[:, -1:, :], "gx", 1)
    diff_x = flow_x - jnp.concatenate([west_row, flow_x[:, :-1]], axis=1)
    source = (diff_x + diff_y + diff_z) / time_step
    flat = jnp.dot(source.reshape(levels * row_count, columns), table_y, precision=highest)
    spectral = lax.all_to_all(
        flat.reshape(levels, row_count, columns), "gx", split_axis=2, concat_axis=1, tiled=True
    )
    modes = jnp.einsum("kx,zxy->zky", table_x, spectral, precision=highest)
    wave_x = jnp.arange(x_total, dtype=jnp.int32).astype(jnp.float32)
    wave_y = (lax.axis_index("gx") * y_slab + jnp.arange(y_slab, dtype=jnp.int32)).astype(
        jnp.float32
    )
    eigen = (
        4.0 * jnp.square(jnp.sin(wave_x * (math.pi / x_total)))[:, None]
        + 4.0 * jnp.square(jnp.sin(wave_y * (math.pi / columns)))[None, :]
    )
    solved = jnp.stack(thomas([modes[level] for level in range(levels)], eigen), axis=0)
    physical = jnp.einsum("kx,zxy->zky", table_x, solved, precision=highest) / x_total
    flat = (
        jnp.dot(
            lax.all_to_all(physical, "gx", split_axis=1, concat_axis=2, tiled=True).reshape(
                levels * row_count, columns
            ),
            table_y,
            precision=highest,
        )
        / columns
    )
    pressure = flat.reshape(levels, row_count, columns)
    east_row = from_behind(pressure[:, :1, :], "gx", -1)
    grad_x = jnp.concatenate([pressure[:, 1:], east_row], axis=1) - pressure
    grad_y = jnp.roll(pressure, -1, axis=2) - pressure
    grad_z = jnp.concatenate([pressure[1:], jnp.zeros_like(pressure[:1])], axis=0) - pressure
    updated = fluid_mask * (coupled - time_step * jnp.stack([grad_x, grad_y, grad_z], axis=0))
    return (updated[None], pressure[None])


def solution(mesh):
    return jax.shard_map(
        local,
        mesh=mesh,
        in_specs=(
            P("nest", None, None, "gx", None),
            P("nest", None, "gx", None),
            P("nest", "gx", None),
            P(),
            P(),
        ),
        out_specs=(P("nest", None, None, "gx", None), P("nest", None, "gx", None)),
        check_vma=False,
    )
```

profile of v0, /device:TPU:1, one launch (start us, length us, event | category | flops | bytes accessed | tf_op | source)
XLA Modules:
  0.0 654.6 jit_solution(828215748368657012)
XLA Ops:
  25.1 9.6 %fusion.51 = f32[3,8,16,2048]{3,2,1,0:T(8,128)} fusion(f32[3,8,16,2048]{3,2,1,0:T(8,128)S(1)} %bitcast.175, f32[3,7,16,2048]{3,2,1,0:T(8,128)} %get-tuple-element.20, f32[3,7,16,2048]{3,2,1,0:T(8,128)} %get-tuple-element.19, f32[3,8,16,2047]{3,2,1,0:T(8,128)S(1)} %copy-done.3, f32[3,8,16,1]{3,2,1,0:T(8,128)} %get-tuple-element.18, ...), kind=kLoop, calls=%fused_computation.70 | loop fusion | flops 28311552 | bytes 30146560 | tf_op jit(solution)/shard_map/mul | solution.py:118
  34.7 13.9 %fusion.63 = f32[3,16,8,1024]{3,1,2,0:T(8,128)S(1)} fusion(f32[3,8,16,2048]{3,2,1,0:T(8,128)} %fusion.51, s32[1024]{0:T(1024)S(1)} %add_select_fusion.5, s32[2048]{0:T(1024)S(1)} %get-tuple-element.40, pred[]{:T(512)S(6)} %eq.44), kind=kOutput, calls=%fused_computation.93 | convolution fusion | flops 9674162176 | bytes 4730881 | tf_op jit(solution)/shard_map/czxy,yj->cxzj/dot_general | solution.py:127
  48.6 7.0 %copy.32 = f32[3,16,8,1024]{1,2,0,3:T(8,128)} copy(f32[3,16,8,1024]{3,1,2,0:T(8,128)S(1)} %fusion.63) | data formatting | bytes 3145728 | tf_op jit(solution)/shard_map/czxy,yj->cxzj/transpose | solution.py:127
  55.6 9.9 %reshape.728 = f32[64,1,6144]{2,1,0:T(1,128)} reshape(f32[1024,3,8,16]{3,2,1,0:T(8,128)} %bitcast.181) | data formatting | bytes 3145728
  65.5 9.6 %all-to-all-start = ((f32[64,1,6144]{2,1,0:T(1,128)}), f32[64,1,6144]{2,1,0:T(1,128)S(1)}, u32[]{:S(2)}, u32[]{:S(2)}) async-start(f32[64,1,6144]{2,1,0:T(1,128)} %reshape.728), calls=%async_computation | async-start | bytes 3145728 | tf_op jit(solution)/shard_map/all_to_all | solution.py:128
  75.7 22.1 %all-to-all-done = f32[64,1,6144]{2,1,0:T(1,128)S(1)} async-done(((f32[64,1,6144]{2,1,0:T(1,128)}), f32[64,1,6144]{2,1,0:T(1,128)S(1)}, u32[]{:S(2)}, u32[]{:S(2)}) %all-to-all-start) | async-done | bytes 1572896 | tf_op jit(solution)/shard_map/all_to_all | solution.py:128
  102.9 7.0 %reshape.729 = f32[1024,3,8,16]{3,2,1,0:T(8,128)} reshape(f32[64,6144]{1,0:T(8,128)S(1)} %reduce) | data formatting | bytes 3145728
  109.9 16.5 %copy.35 = f32[3,64,16,8,16]{2,1,4,3,0:T(8,128)} copy(f32[3,64,16,8,16]{2,3,0,4,1:T(8,128)} %bitcast.176) | data formatting | bytes 3145728 | tf_op jit(solution)/shard_map/all_to_all | solution.py:128
  126.3 12.9 %copy.34 = f32[3,64,16,8,16]{4,3,2,1,0:T(8,128)} copy(f32[3,64,16,8,16]{2,3,0,4,1:T(8,128)} %bitcast.177) | data formatting | bytes 3145728 | tf_op jit(solution)/shard_map/all_to_all | solution.py:128
  139.2 11.0 %all_to_all.53 = f32[3,1024,8,16]{1,3,2,0:T(8,128)S(1)} reshape(f32[3,64,16,8,16]{2,1,4,3,0:T(8,128)} %copy.35) | data formatting | bytes 3145728 | tf_op jit(solution)/shard_map/all_to_all | solution.py:128
  151.2 8.8 %copy.36 = f32[3,512,2,8,16]{4,3,2,1,0:T(8,128)} copy(f32[3,512,2,8,16]{1,4,3,0,2:T(8,128)S(1)} %pad_maximum_fusion.9) | data formatting | bytes 3145728 | tf_op jit(solution)/shard_map/stack | solution.py:132
  160.0 6.9 %broadcast_in_dim.18 = f32[3,1024,8,16]{3,2,1,0:T(8,128)} broadcast(f32[]{:T(128)} %constant.125.clone.1), dimensions={} | broadcast | bytes 1572868 | tf_op jit(solution)/shard_map/broadcast_in_dim | solution.py:136
  167.0 8.0 %fusion.23 = f32[3,1024,8,16]{3,2,1,0:T(8,128)} fusion(f32[3,1024,8,16]{3,2,1,0:T(8,128)} %broadcast_in_dim.18, s32[]{:T(128)S(6)} %select_n.126, f32[3,512,2,8,16]{4,3,2,1,0:T(8,128)} %bitcast.184), kind=kLoop, calls=%fused_computation.34 | loop fusion | flops 393216 | bytes 18874372 | tf_op jit(solution)/shard_map/dynamic_update_slice | solution.py:135
  180.0 7.4 %copy.37 = f32[3,1024,8,16]{1,3,2,0:T(8,128)S(1)} copy(f32[3,1024,8,16]{3,2,1,0:T(8,128)} %broadcast_select_fusion) | data formatting | bytes 3145728 | tf_op jit(solution)/shard_map/jit(_where)/select_n | solution.py:138
  187.5 8.1 %collective-permute-start.2 = (f32[3,1024,8,16]{1,3,2,0:T(8,128)S(1)}, f32[3,1024,8,16]{1,3,2,0:T(8,128)S(1)}, u32[]{:S(2)}, u32[]{:S(2)}) collective-permute-start(f32[3,1024,8,16]{1,3,2,0:T(8,128)S(1)} %copy.37), channel_id=1, source_target_pairs={{0,64},{64,0},{1,65},{65,1},{2,66},{66,2},{3,67},{67,3},{4,68},{68... | collective-permute-start | bytes 4718600 | tf_op jit(solution)/shard_map/ppermute | solution.py:32
  195.6 33.9 %collective-permute-done.2 = f32[3,1024,8,16]{1,3,2,0:T(8,128)S(1)} collective-permute-done((f32[3,1024,8,16]{1,3,2,0:T(8,128)S(1)}, f32[3,1024,8,16]{1,3,2,0:T(8,128)S(1)}, u32[]{:S(2)}, u32[]{:S(2)}) %collective-permute-start.2) | collective-permute-done | bytes 1572896 | tf_op jit(solution)/shard_map/ppermute | solution.py:32
  229.5 7.0 %copy.38 = f32[3,1024,8,16]{3,2,0,1:T(8,128)} copy(f32[3,1024,8,16]{1,3,2,0:T(8,128)S(1)} %collective-permute-done.2) | data formatting | bytes 3145728 | tf_op jit(solution)/shard_map/ppermute | solution.py:32
  236.4 9.7 %reshape.730 = f32[64,1,6144]{2,1,0:T(1,128)} reshape(f32[1024,3,8,16]{3,2,1,0:T(8,128)} %bitcast.182) | data formatting | bytes 3145728
  252.1 22.5 %all-to-all-done.1 = f32[64,1,6144]{2,1,0:T(1,128)S(1)} async-done(((f32[64,1,6144]{2,1,0:T(1,128)}), f32[64,1,6144]{2,1,0:T(1,128)S(1)}, u32[]{:S(2)}, u32[]{:S(2)}) %all-to-all-start.1) | async-done | bytes 1572896 | tf_op jit(solution)/shard_map/all_to_all | solution.py:140
  285.9 16.4 %copy.58 = f32[3,16,8,64,16]{4,3,1,2,0:T(8,128)} copy(f32[3,16,8,64,16]{4,2,0,1,3:T(8,128)} %bitcast.183) | data formatting | bytes 3145728 | tf_op jit(solution)/shard_map/all_to_all | solution.py:140
  302.2 12.0 %reshape.727 = f32[3,16,8,1024]{3,1,2,0:T(8,128)} reshape(f32[3,16,8,64,16]{4,3,1,2,0:T(8,128)} %copy.58) | data formatting | bytes 3145728 | tf_op jit(solution)/shard_map/all_to_all | solution.py:140
  314.2 22.1 %select_multiply_fusion = f32[3,8,16,2048]{3,2,1,0:T(8,128)S(1)} fusion(f32[3,8,16,2048]{3,2,1,0:T(8,128)} %fusion.51, f32[3,16,8,1024]{3,1,2,0:T(8,128)} %reshape.727, s32[2048]{0:T(1024)S(1)} %get-tuple-element.39, s32[2048]{0:T(1024)S(1)} %add_minimum_fusion, s32[2048]{0:T(1024)S(1)} %get-tuple-element.40, pred[2048]{0:T(1024)(128)(4,1)S(1)} %fusion.114, ...), kind=kOutput, calls=%fused_computation.86 | convolution fusion | flops 9690939392 | bytes 9103361 | tf_op jit(solution)/shard_map/cxzj,jy->czxy/dot_general | solution.py:150
  340.1 76.4 %fusion.3 = f32[8,16,2048]{2,1,0:T(8,128)} fusion(f32[8,16,2048]{2,1,0:T(8,128)S(1)} %fusion.175), kind=kOutput, calls=%fused_computation.6 | convolution fusion | flops 6505365504 | bytes 2097152 | tf_op jit(solution)/shard_map/dot_general | solution.py:172
  422.5 6.9 %reshape.732 = f32[64,1,4096]{2,1,0:T(1,128)} reshape(f32[2048,8,16]{2,1,0:T(8,128)} %bitcast.192) | data formatting | bytes 2097152
  429.4 11.4 %all-to-all-start.2 = ((f32[64,1,4096]{2,1,0:T(1,128)}), f32[64,1,4096]{2,1,0:T(1,128)}, u32[]{:S(2)}, u32[]{:S(2)}) async-start(f32[64,1,4096]{2,1,0:T(1,128)} %reshape.732), calls=%async_computation.2 | async-start | bytes 2097152 | tf_op jit(solution)/shard_map/all_to_all | solution.py:173
  440.9 17.5 %fusion.178 = f32[1024,1024,1]{1,0,2:T(8,128)} fusion(), kind=kLoop, calls=%fused_computation.45.clone.clone.clone.1 | loop fusion | flops 15728640 | bytes 4194304 | tf_op jit(solution)/shard_map/kx,zxy->zky/dot_general | solution.py:176
  470.1 6.9 %copy.44 = f32[8,64,16,32]{3,2,1,0:T(8,128)} copy(f32[8,64,16,32]{2,0,3,1:T(8,128)} %bitcast.193) | data formatting | bytes 2097152 | tf_op jit(solution)/shard_map/all_to_all | solution.py:173
  477.0 28.5 %fusion.66 = f32[8,1024,32]{1,2,0:T(8,128)S(1)} fusion(f32[8,1024,32]{2,1,0:T(8,128)} %bitcast.194, f32[1024,1024,1]{1,0,2:T(8,128)} %fusion.178), kind=kOutput, calls=%fused_computation.94 | convolution fusion | flops 3221225472 | bytes 6291456 | tf_op jit(solution)/shard_map/kx,zxy->zky/dot_general | solution.py:176
  507.0 21.7 %fusion.72 = f32[8,1024,32]{1,2,0:T(8,128)} fusion(f32[8,1024,32]{1,2,0:T(8,128)S(1)} %divide_dynamic-update-slice_fusion), kind=kOutput, calls=%fused_computation.96 | convolution fusion | flops 3237216256 | bytes 2097152 | tf_op jit(solution)/shard_map/kx,zxy->zky/dot_general | solution.py:186
  537.0 9.6 %all-to-all-start.3 = ((f32[64,1,4096]{2,1,0:T(1,128)}), f32[64,1,4096]{2,1,0:T(1,128)}, u32[]{:S(2)}, u32[]{:S(2)}) async-start(f32[64,1,4096]{2,1,0:T(1,128)} %reshape.734), calls=%async_computation.3 | async-start | bytes 2097152 | tf_op jit(solution)/shard_map/all_to_all | solution.py:189
  546.6 67.1 %sine_add_fusion.10 = f32[2048,2048]{1,0:T(8,128)} fusion(), kind=kLoop, calls=%fused_computation.8.clone.clone.clone.clone.1 | loop fusion | flops 62914560 | bytes 16777216 | tf_op jit(solution)/shard_map/dot_general | solution.py:188
  633.9 13.2 %fusion.61 = f32[128,2048]{1,0:T(8,128)S(1)} fusion(f32[128,2048]{1,0:T(8,128)} %reshape.720, f32[2048,2048]{1,0:T(8,128)} %sine_add_fusion.10), kind=kOutput, calls=%fused_computation.87 | convolution fusion | flops 6442713088 | bytes 18874368 | tf_op jit(solution)/shard_map/dot_general | solution.py:188
  (93 shorter events, 110.3 us)
Async XLA Ops:
  0.6 6.6 %copy-start = (f32[1,3,8,16,2048]{4,3,2,1,0:T(8,128)S(1)}, f32[1,3,8,16,2048]{4,3,2,1,0:T(8,128)}, u32[]{:S(2)}) copy-start(f32[1,3,8,16,2048]{4,3,2,1,0:T(8,128)} %param.5) | copy-start | bytes 9437188
  4.2 14.3 %collective-permute-start = (f32[4,8,1,2048]{3,2,1,0:T(1,128)}, f32[4,8,1,2048]{3,2,1,0:T(1,128)S(1)}, u32[]{:S(2)}, u32[]{:S(2)}) collective-permute-start(f32[4,8,1,2048]{3,2,1,0:T(1,128)} %get-tuple-element.9), channel_id=1, source_target_pairs={{0,1},{1,2},{2,3},{3,4},{4,5},{5,6},{6,7},{7,8},{8,9},{9,10},{10,1... | collective-permute-start | bytes 786440 | tf_op jit(solution)/shard_map/ppermute | solution.py:20
  7.2 11.3 %collective-permute-start.1 = (f32[4,8,1,2048]{3,2,1,0:T(1,128)}, f32[4,8,1,2048]{3,2,1,0:T(1,128)}, u32[]{:S(2)}, u32[]{:S(2)}) collective-permute-start(f32[4,8,1,2048]{3,2,1,0:T(1,128)} %get-tuple-element.8), channel_id=1, source_target_pairs={{1,0},{2,1},{3,2},{4,3},{5,4},{6,5},{7,6},{8,7},{9,8},{10,9},{11,1... | collective-permute-start | bytes 786440 | tf_op jit(solution)/shard_map/ppermute | solution.py:22
  14.2 1.7 copy-start.5
  20.8 4.0 copy-start.2
  20.8 4.3 copy-start.3
  65.5 32.3 %all-to-all-start = ((f32[64,1,6144]{2,1,0:T(1,128)}), f32[64,1,6144]{2,1,0:T(1,128)S(1)}, u32[]{:S(2)}, u32[]{:S(2)}) async-start(f32[64,1,6144]{2,1,0:T(1,128)} %reshape.728), calls=%async_computation | async-start | bytes 3145728 | tf_op jit(solution)/shard_map/all_to_all | solution.py:128
  160.0 14.9 %slice-start = ((s8[12582912]{0:T(1024)(128)(4,1)}), s8[4194304]{0:T(1024)(128)(4,1)S(1)}, s32[]{:S(2)}) async-start(s8[12582912]{0:T(1024)(128)(4,1)} %bitcast.178), calls=%async_computation.4 | async-start | bytes 8388608
  160.0 14.9 %slice-start.1 = ((s8[12582912]{0:T(1024)(128)(4,1)}), s8[4194304]{0:T(1024)(128)(4,1)S(1)}, s32[]{:S(2)}) async-start(s8[12582912]{0:T(1024)(128)(4,1)} %bitcast.178), calls=%async_computation.5 | async-start | bytes 8388608
  167.0 8.0 %slice-start.2 = ((s8[12582912]{0:T(1024)(128)(4,1)}), s8[4194304]{0:T(1024)(128)(4,1)S(1)}, s32[]{:S(2)}) async-start(s8[12582912]{0:T(1024)(128)(4,1)} %bitcast.178), calls=%async_computation.6 | async-start | bytes 8388608
  187.5 42.0 %collective-permute-start.2 = (f32[3,1024,8,16]{1,3,2,0:T(8,128)S(1)}, f32[3,1024,8,16]{1,3,2,0:T(8,128)S(1)}, u32[]{:S(2)}, u32[]{:S(2)}) collective-permute-start(f32[3,1024,8,16]{1,3,2,0:T(8,128)S(1)} %copy.37), channel_id=1, source_target_pairs={{0,64},{64,0},{1,65},{65,1},{2,66},{66,2},{3,67},{67,3},{4,68},{68... | collective-permute-start | bytes 4718600 | tf_op jit(solution)/shard_map/ppermute | solution.py:32
  246.2 28.5 %all-to-all-start.1 = ((f32[64,1,6144]{2,1,0:T(1,128)}), f32[64,1,6144]{2,1,0:T(1,128)S(1)}, u32[]{:S(2)}, u32[]{:S(2)}) async-start(f32[64,1,6144]{2,1,0:T(1,128)} %reshape.730), calls=%async_computation.1 | async-start | bytes 3145728 | tf_op jit(solution)/shard_map/all_to_all | solution.py:140
  336.6 2.8 collective-permute-start.3
  429.4 29.0 %all-to-all-start.2 = ((f32[64,1,4096]{2,1,0:T(1,128)}), f32[64,1,4096]{2,1,0:T(1,128)}, u32[]{:S(2)}, u32[]{:S(2)}) async-start(f32[64,1,4096]{2,1,0:T(1,128)} %reshape.732), calls=%async_computation.2 | async-start | bytes 2097152 | tf_op jit(solution)/shard_map/all_to_all | solution.py:173
  537.0 76.7 %all-to-all-start.3 = ((f32[64,1,4096]{2,1,0:T(1,128)}), f32[64,1,4096]{2,1,0:T(1,128)}, u32[]{:S(2)}, u32[]{:S(2)}) async-start(f32[64,1,4096]{2,1,0:T(1,128)} %reshape.734), calls=%async_computation.3 | async-start | bytes 2097152 | tf_op jit(solution)/shard_map/all_to_all | solution.py:189
  647.1 4.4 copy-start.1
  647.7 3.8 collective-permute-start.4
  648.3 3.5 copy-start.4
where the time goes:
time: 664 us; the launch traced here: 655 us
  local copies, waits for them, and re-layouts  201 us (30%)
  matrix products  176 us (27%)
  other arithmetic  143 us (22%)
  waiting for transfers between devices  82.9 us (12%)
  starting transfers between devices  49.2 us (7%)
    dot_general x1, matrix products, local(): jnp.dot(source.reshape(levels * row_count, columns), table_y, precision=h...  76.4 us
    dot_general x1, other arithmetic, local(): jnp.dot(lax.all_to_all(physical, 'gx', split_axis=1, concat_axis=2, tiled...  67.1 us
    unnamed x28, local copies, waits for them, and re-layouts  55.3 us
    all_to_all x4, local copies, waits for them, and re-layouts, local(): lax.all_to_all(outgoing, 'gx', split_axis=3, concat_axis=1, tiled=True)  41 us
    ppermute x1, waiting for transfers between devices, swapped(): return lax.ppermute(value, axis, pairs)  33.9 us
    dot_general x1, matrix products, local(): modes = jnp.einsum('kx,zxy->zky', table_x, spectral, precision=highest)  28.5 us
    all_to_all x2, local copies, waits for them, and re-layouts, local(): lax.all_to_all(received, 'gx', split_axis=1, concat_axis=3, tiled=True)  28.3 us
    all_to_all x1, waiting for transfers between devices, local(): lax.all_to_all(received, 'gx', split_axis=1, concat_axis=3, tiled=True)  22.5 us
  transfers between devices with their start and end apart: 9, of which 5 were waited for; matrix products, arithmetic and copies ran while one was open for 15% of the time, Pallas kernels for 0%

commit v1 on v0

v1 whole, which is shorter than its diff:
```python
import functools
import math

import jax
import jax.numpy as jnp
import ml_dtypes
import numpy as np
from jax import lax
from jax.experimental import pallas as pl
from jax.experimental.pallas import tpu as pltpu
from jax.sharding import PartitionSpec as P

LEVELS = 8
ROWS = 16
LANES = 128
EXTRA = 144
DT = 0.2
BLEND = 0.5
f32 = jnp.float32
bf16 = jnp.bfloat16
VMEM_SPEC = pl.BlockSpec(memory_space=pltpu.VMEM)
SMEM_SPEC = pl.BlockSpec(memory_space=pltpu.SMEM)
ANY_SPEC = pl.BlockSpec(memory_space=pl.ANY)
PARAMS = dict(vmem_limit_bytes=50 * 1024 * 1024)


def split_np(table):
    high = table.astype(ml_dtypes.bfloat16)
    low = (table - high.astype(np.float64)).astype(ml_dtypes.bfloat16)
    return high, low


def split(value):
    high = value.astype(bf16)
    low = (value - high.astype(f32)).astype(bf16)
    return high, low


def cas(angle):
    return np.cos(angle) + np.sin(angle)


@functools.lru_cache(maxsize=None)
def tables(x_total, columns, group):
    half = columns // 2
    m = np.arange(half)
    even = cas(2 * np.pi * ((m[:, None] * m[None, :]) % half) / half)
    odd_index = ((2 * m[:, None] + 1) * (2 * m[None, :] + 1)) % (2 * columns)
    odd = cas(2 * np.pi * odd_index / (2 * columns))
    even_high, even_low = split_np(even)
    odd_high, odd_low = split_np(odd)
    y_tables = np.stack([even_high, even_low, odd_high, odd_low])
    j = np.arange(LEVELS)
    z_vectors = math.sqrt(4 / 17) * np.cos((2 * j[:, None] + 1) * (2 * j[None, :] + 1) * np.pi / 34)
    z_values = 2 - 2 * np.cos((2 * j + 1) * np.pi / 17)
    turn = np.zeros((EXTRA, EXTRA))
    for x in range(ROWS + 1):
        for level in range(LEVELS):
            place = level * ROWS + x if x < ROWS else ROWS * LEVELS + level
            turn[x * LEVELS : x * LEVELS + LEVELS, place] = z_vectors[:, level]
    turn_high, turn_low = split_np(turn)
    back_high, back_low = split_np(turn.T)
    turn_stack = np.concatenate([turn_high, turn_low])
    back_stack = np.concatenate([back_high, back_low])
    wave = np.concatenate([2 * m, 2 * m + 1])
    mu = 4 * np.sin(np.pi * wave / columns)[None, :] ** 2 + z_values[:, None]
    root = 1 + mu / 2 - np.sqrt(mu + mu * mu / 4)
    scale = -1 / (1 / root - root) / columns
    modes = np.stack([root, scale]).astype(np.float32)
    reach = root**ROWS
    tiles = columns // LANES
    jump = np.stack([reach, 1 / (1 - reach**group)])
    jump = jump.reshape(2, LEVELS, tiles, LANES).transpose(2, 0, 1, 3).astype(np.float32)
    wide = np.zeros((2, 256, 256))
    for y in range(256):
        if y % 2 == 0:
            wide[:, y // 2, y] = 1
        else:
            wide[:, y // 2, y] = 0.5
            wide[0, y // 2 + 1, y] = 0.5
            wide[1, min(y // 2 + 1, 127), y] += 0.5
    pair = np.zeros((256, LANES))
    pair[np.arange(256), np.arange(256) // 2] = 0.5
    return dict(
        y=y_tables,
        turn=turn_stack,
        back=back_stack,
        modes=modes,
        jump=jump,
        wide=wide.astype(ml_dtypes.bfloat16),
        pair=pair.astype(ml_dtypes.bfloat16),
    )


def mxu(left, right):
    return jnp.dot(left, right, preferred_element_type=f32)


def halo_kernel(vel, visc, west, east, edge, sems):
    me = lax.axis_index("gx")
    group = lax.axis_size("gx")
    for c in range(3):
        edge[0, c] = vel[c, :, 0, :]
        edge[1, c] = vel[c, :, ROWS - 1, :]
    edge[0, 3] = visc[:, 0, :]
    edge[1, 3] = visc[:, ROWS - 1, :]
    right = lax.rem(me + 1, group)
    left = lax.rem(me + group - 1, group)
    to_right = pltpu.make_async_remote_copy(
        edge.at[1], west, sems.at[0], sems.at[1], device_id={"gx": right},
        device_id_type=pl.DeviceIdType.MESH,
    )
    to_left = pltpu.make_async_remote_copy(
        edge.at[0], east, sems.at[2], sems.at[3], device_id={"gx": left},
        device_id_type=pl.DeviceIdType.MESH,
    )
    to_right.start()
    to_left.start()
    to_right.wait()
    to_left.wait()


def stencil_kernel(oy_ref, vel, visc, heights, west, east, pair, prov, out, mean, tile):
    columns = vel.shape[-1]
    tiles = columns // LANES
    blocks = columns // 256
    is_child = lax.axis_index("nest") == 1
    row = lax.broadcasted_iota(jnp.int32, (ROWS, 256), 0)
    lane = lax.broadcasted_iota(jnp.int32, (ROWS, LANES), 1)

    def cell(i, carry):
        z = i // blocks
        start = pl.multiple_of(lax.rem(i, blocks) * 256, 256)
        here = pl.ds(start, 256)
        before = pl.ds(pl.multiple_of(lax.rem(start + columns - LANES, columns), LANES), LANES)
        after = pl.ds(pl.multiple_of(lax.rem(start + 256, columns), LANES), LANES)
        up = jnp.minimum(z + 1, LEVELS - 1)
        down = jnp.maximum(z - 1, 0)
        up_open = jnp.where(z < LEVELS - 1, 1.0, 0.0).astype(f32)
        down_open = jnp.where(z > 0, 1.0, 0.0).astype(f32)

        def around(ref, lead, c):
            mid = ref[lead + (z, slice(None), here)]
            wide = jnp.concatenate(
                [ref[lead + (z, slice(None), before)], mid, ref[lead + (z, slice(None), after)]],
                axis=1,
            )
            north = pltpu.roll(wide, 511, 1)[:, LANES : LANES + 256]
            south = pltpu.roll(wide, 1, 1)[:, LANES : LANES + 256]
            plus = jnp.where(row == ROWS - 1, east[c, pl.ds(z, 1), here], pltpu.roll(mid, ROWS - 1, 0))
            minus = jnp.where(row == 0, west[c, pl.ds(z, 1), here], pltpu.roll(mid, 1, 0))
            top = ref[lead + (up, slice(None), here)]
            bottom = ref[lead + (down, slice(None), here)]
            return mid, plus, minus, north, south, top, bottom

        k, ke, kw, kn, ks, kt, kb = around(visc, (), 3)
        flow = [around(vel, (c,), c) for c in range(3)]
        half = 0.5 * DT
        kh = half * k
        b0, b1, b2 = (half * flow[c][0] for c in range(3))
        ae = (kh + half * ke) - b0
        aw = (kh + half * kw) + b0
        an = (kh + half * kn) - b1
        as_ = (kh + half * ks) + b1
        at = (kh + half * kt) - b2
        ab = (kh + half * kb) + b2
        mask = jnp.where(z >= heights[:, here], 1.0, 0.0).astype(f32)
        own = 1.0 - (((ae + aw) + (an + as_)) + (at + ab))
        at = at * up_open
        ab = ab * down_open
        for c in range(3):
            mid, plus, minus, north, south, top, bottom = flow[c]
            value = own * mid + ae * plus + aw * minus + an * north + as_ * south + at * top + ab * bottom
            prov[c, z, :, here] = value * mask
        return carry

    lax.fori_loop(0, LEVELS * blocks, cell, 0)

    @pl.when(jnp.logical_not(is_child))
    def _():
        oy = oy_ref[0]
        first = oy // LANES
        shift = lax.rem(oy, LANES)
        turn = lax.rem(LANES - shift, LANES)

        def unit(i, carry):
            cz = i // blocks
            b = lax.rem(i, blocks)
            c = cz // LEVELS
            z = lax.rem(cz, LEVELS)
            one = pl.ds(pl.multiple_of(lax.rem(first + b, tiles) * LANES, LANES), LANES)
            two = pl.ds(pl.multiple_of(lax.rem(first + b + 1, tiles) * LANES, LANES), LANES)
            low = pltpu.roll(prov[c, z, :, one], turn, 1)
            high = pltpu.roll(prov[c, z, :, two], turn, 1)
            out[b * 8 + cz // 3, lax.rem(cz, 3)] = jnp.where(lane < LANES - shift, low, high)
            return carry

        lax.fori_loop(0, 24 * blocks, unit, 0)

    @pl.when(is_child)
    def _():
        def rows(cz, carry):
            c = cz // LEVELS
            z = lax.rem(cz, LEVELS)
            for t in range(tiles):
                cols = pl.ds(t * LANES, LANES)
                tile[t] = prov[c, z, :, cols]
                evens = tile[t, pl.ds(0, 8, stride=2), :]
                odds = tile[t, pl.ds(1, 8, stride=2), :]
                mean[pl.ds(pl.multiple_of(cz * 8, 8), 8), cols] = 0.5 * (evens + odds)
            return carry

        lax.fori_loop(0, 24, rows, 0)
        for b in range(blocks):
            high, low = split(mean[:, pl.ds(b * 256, 256)])
            value = mxu(high, pair[...]) + mxu(low, pair[...])
            out[pl.ds(b * 8, 8), :, pl.ds(0, 8), :] = value.reshape(8, 3, 8, LANES)


def remote(src, dst, send, recv, nest, k):
    return pltpu.make_async_remote_copy(
        src, dst, send, recv, device_id={"nest": nest, "gx": k},
        device_id_type=pl.DeviceIdType.MESH,
    )


def await_bytes(ref, sem):
    pltpu.make_async_copy(ref, ref, sem).wait()


def gather_kernel(src, under, above, sems):
    group = src.shape[0]
    x_total = group * ROWS
    half = x_total // 2
    me = lax.axis_index("gx")
    nest = lax.axis_index("nest")
    here = pl.ds(pl.multiple_of(me * ROWS, ROWS), ROWS)

    @pl.when(nest == 0)
    def _():
        def send_rows(i, carry):
            k = lax.rem(me + i, group)
            remote(src.at[k], under.at[:, here], sems.at[0], sems.at[1], 0, k).start()
            return carry

        lax.fori_loop(1, group, send_rows, 0)
        pltpu.make_async_copy(src.at[me], under.at[:, here], sems.at[1]).start()
        blank = jnp.zeros((3, ROWS, LANES), f32)
        under[:, pl.ds(x_total, ROWS)] = blank
        above[:, pl.ds(0, ROWS)] = blank
        above[:, pl.ds(ROWS + half, ROWS)] = blank
        above[:, pl.ds(2 * ROWS + half, ROWS)] = blank
        await_bytes(src.at[pl.ds(0, group - 1)], sems.at[0])
        await_bytes(under.at[:, pl.ds(0, x_total)], sems.at[1])
        await_bytes(above.at[:, pl.ds(ROWS, half)], sems.at[2])

    @pl.when(nest == 1)
    def _():
        slot = pl.ds(pl.multiple_of(ROWS + me * 8, 8), 8)

        def send_means(i, carry):
            k = lax.rem(me + i, group)
            remote(src.at[k, :, pl.ds(0, 8)], above.at[:, slot], sems.at[0], sems.at[2], 0, k).start()
            return carry

        lax.fori_loop(0, group, send_means, 0)
        await_bytes(src.at[:, :, pl.ds(0, 8)], sems.at[0])


def shift_kernel(ox_ref, under, above, to_child, to_parent):
    group = to_child.shape[0]
    half = group * ROWS // 2

    @pl.when(lax.axis_index("nest") == 0)
    def _():
        ox = ox_ref[0]

        def fill(g, carry):
            rows = pl.ds(pl.multiple_of((ox // 8 + g) * 8, 8), 16)
            first = jnp.clip(ROWS * g - ox + ROWS, 0, half + ROWS)
            back = pl.ds(pl.multiple_of(first // 8 * 8, 8), 24)
            for u in range(3):
                moved = pltpu.roll(under[u, rows], lax.rem(16 - lax.rem(ox, 8), 16), 0)
                to_child[g, pl.ds(u * 9, 9)] = moved[:9]
                moved = pltpu.roll(above[u, back], lax.rem(24 - lax.rem(first, 8), 24), 0)
                to_parent[g, pl.ds(u * ROWS, ROWS)] = moved[:ROWS]
            return carry

        lax.fori_loop(0, group, fill, 0)


def scatter_kernel(to_child, to_parent, dst, sems):
    group = to_child.shape[0]
    me = lax.axis_index("gx")
    nest = lax.axis_index("nest")

    @pl.when(nest == 0)
    def _():
        def send(i, carry):
            k = lax.rem(me + i, group)
            remote(to_child.at[k], dst.at[me, pl.ds(0, 32)], sems.at[0], sems.at[1], 1, k).start()

            @pl.when(i > 0)
            def _():
                remote(to_parent.at[k], dst.at[me], sems.at[2], sems.at[1], 0, k).start()

            return carry

        lax.fori_loop(0, group, send, 0)
        pltpu.make_async_copy(to_parent.at[me], dst.at[me], sems.at[1]).start()
        await_bytes(to_child, sems.at[0])
        await_bytes(to_parent.at[pl.ds(0, group - 1)], sems.at[2])
        await_bytes(dst, sems.at[1])

    @pl.when(nest == 1)
    def _():
        await_bytes(dst.at[:, pl.ds(0, 32)], sems.at[1])


def forward_kernel(
    ox_ref, oy_ref, prov, got, heights, wide_t, turn_t, modes, y_any,
    coupled, spectrum, ends, y_t, mapped, wide, rate, source, turned, sem,
):
    columns = prov.shape[-1]
    group = got.shape[0]
    x_total = group * ROWS
    half = columns // 2
    tiles = columns // LANES
    blocks = columns // 256
    load = pltpu.make_async_copy(y_any, y_t, sem)
    load.start()
    me = lax.axis_index("gx")
    is_child = lax.axis_index("nest") == 1
    ox = ox_ref[0]
    oy = oy_ref[0]
    lane = lax.broadcasted_iota(jnp.int32, (ROWS, LANES), 1)
    row = lax.broadcasted_iota(jnp.int32, (ROWS, LANES), 0)

    @pl.when(is_child)
    def _():
        for b in range(blocks):
            left = got[pl.ds(b * 8, 8), pl.ds(0, 32), :].reshape(256, LANES)
            nxt = min(b + 1, blocks - 1)
            right = got[pl.ds(nxt * 8, 8), pl.ds(0, 32), :].reshape(256, LANES)
            high, low = split(jnp.concatenate([left, right], axis=1))
            table = wide_t[0 if b < blocks - 1 else 1]
            wide[:, :, pl.ds(b * 256, 256)] = (mxu(high, table) + mxu(low, table)).reshape(8, 32, 256)
        last = me == group - 1

        def unit(kz, carry):
            for u in range(3):
                cz = kz * 3 + u
                for t in range(tiles):
                    cols = pl.ds(t * LANES, LANES)
                    own = wide[kz, pl.ds(u * 9, 8), cols]
                    after = wide[kz, pl.ds(u * 9 + 1, 8), cols]
                    tail = lax.broadcasted_iota(jnp.int32, (8, LANES), 0) == 7
                    after = jnp.where(jnp.logical_and(tail, last), own, after)
                    mapped[cz, t, pl.ds(0, 8, stride=2), :] = own
                    mapped[cz, t, pl.ds(1, 8, stride=2), :] = 0.5 * (own + after)
            return carry

        lax.fori_loop(0, 8, unit, 0)

        def rates(t, carry):
            cols = pl.ds(pl.multiple_of(t * LANES, LANES), LANES)
            x = me * ROWS + row
            y = t * LANES + lane
            near_y = jnp.minimum(y, columns - 1 - y)
            near_x = jnp.minimum(x, x_total - 1 - x)
            near = jnp.minimum(near_x, near_y).astype(f32)
            rate[:, cols] = 0.2 + 0.8 * jnp.exp(-near * (16.0 / columns))
            return carry

        lax.fori_loop(0, tiles, rates, 0)

    @pl.when(jnp.logical_not(is_child))
    def _():
        first = oy // LANES
        shift = lax.rem(oy, LANES)

        def unit(i, carry):
            cz = i // tiles
            t = lax.rem(i, tiles)
            at = lax.rem(t - first + tiles, tiles)
            low = jnp.minimum(at, blocks - 1)
            high = jnp.minimum(lax.rem(at + tiles - 1, tiles), blocks - 1)
            kz = cz // 3
            rows = pl.ds(pl.multiple_of(lax.rem(cz, 3) * ROWS, ROWS), ROWS)
            one = pltpu.roll(got[low * 8 + kz, rows, :], shift, 1)
            two = pltpu.roll(got[high * 8 + kz, rows, :], shift, 1)
            mapped[cz, t] = jnp.where(lane >= shift, one, two)
            return carry

        lax.fori_loop(0, 24 * tiles, unit, 0)

        def rates(t, carry):
            cols = pl.ds(pl.multiple_of(t * LANES, LANES), LANES)
            x = me * ROWS + row
            y = t * LANES + lane
            j = y - oy
            j = jnp.where(j < 0, j + columns, j)
            inside = (x >= ox) & (x < ox + x_total // 2) & (j < half)
            rate[:, cols] = jnp.where(inside, BLEND, 0.0)
            return carry

        lax.fori_loop(0, tiles, rates, 0)

    source[pl.ds(ROWS * LEVELS, ROWS), :] = jnp.zeros((ROWS, columns), f32)

    def blend(i, carry):
        z = i // blocks
        b = lax.rem(i, blocks)
        cols = pl.ds(pl.multiple_of(b * 256, 256), 256)
        weight = rate[:, cols]
        mask = jnp.where(z >= heights[:, cols], 1.0, 0.0).astype(f32)
        for c in range(3):
            own = prov[c, z, :, cols]
            other = jnp.concatenate([mapped[c * LEVELS + z, 2 * b], mapped[c * LEVELS + z, 2 * b + 1]], axis=1)
            change = jnp.where(weight > 0.0, other - own, 0.0)
            coupled[c, z, :, cols] = (own + weight * change) * mask
        return carry

    lax.fori_loop(0, LEVELS * blocks, blend, 0)
    row2 = lax.broadcasted_iota(jnp.int32, (ROWS, 256), 0)

    def diverge(i, carry):
        z = i // blocks
        start = pl.multiple_of(lax.rem(i, blocks) * 256, 256)
        cols = pl.ds(start, 256)
        before = pl.ds(pl.multiple_of(lax.rem(start + columns - LANES, columns), LANES), LANES)
        flow_x = coupled[0, z, :, cols]
        flow_y = coupled[1, z, :, cols]
        flow_z = coupled[2, z, :, cols]
        beyond = jnp.concatenate([coupled[1, z, :, before], flow_y], axis=1)
        south = pltpu.roll(beyond, 1, 1)[:, LANES:]
        west = jnp.where(row2 == 0, 0.0, pltpu.roll(flow_x, 1, 0))
        under = coupled[2, jnp.maximum(z - 1, 0), :, cols] * jnp.where(z > 0, 1.0, 0.0).astype(f32)
        value = ((flow_x - west) + (flow_y - south)) + (flow_z - under)
        source[pl.ds(pl.multiple_of(z * ROWS, ROWS), ROWS), cols] = value * (1.0 / DT)
        source[pl.ds(ROWS * LEVELS + z, 1), cols] = flow_x[ROWS - 1 :] * (-1.0 / DT)
        return carry

    lax.fori_loop(0, LEVELS * blocks, diverge, 0)

    def turning(b, carry):
        cols = pl.ds(pl.multiple_of(b * 256, 256), 256)
        high, low = split(source[:, cols])
        both = mxu(turn_t[...], high)
        turned[:, cols] = (both[:EXTRA] + both[EXTRA:]) + mxu(turn_t[pl.ds(0, EXTRA), :], low)
        return carry

    lax.fori_loop(0, blocks, turning, 0)
    load.wait()
    width = min(half, 256)
    for part in range(2):
        one = turned[:, pl.ds(0, half)]
        two = turned[:, pl.ds(half, half)]
        high, low = split(one + two if part == 0 else one - two)
        stacked = jnp.concatenate([high, low], axis=0)

        def transform(b, carry):
            cols = pl.ds(pl.multiple_of(b * width, width), width)
            both = mxu(stacked, y_t[2 * part, :, cols])
            value = (both[:EXTRA] + both[EXTRA:]) + mxu(high, y_t[2 * part + 1, :, cols])
            spectrum[:, pl.ds(pl.multiple_of(part * half + b * width, width), width)] = value
            return carry

        lax.fori_loop(0, half // width, transform, 0)

    def scans(t, carry):
        cols = pl.ds(pl.multiple_of(t * LANES, LANES), LANES)
        root = modes[0, :, cols]
        lead = spectrum[pl.ds(0, 8), cols]
        for x in range(1, ROWS + 1):
            lead = spectrum[pl.ds(8 * x, 8), cols] + root * lead
        trail = spectrum[pl.ds(8 * ROWS, 8), cols]
        for x in range(ROWS - 1, -1, -1):
            trail = spectrum[pl.ds(8 * x, 8), cols] + root * trail
        ends[t] = lead
        ends[tiles + t] = trail
        return carry

    lax.fori_loop(0, tiles, scans, 0)


def chain_kernel(ends, jump, dst, held, result, sems):
    me = lax.axis_index("gx")
    nest = lax.axis_index("nest")
    group = held.shape[0]
    count = ends.shape[0]
    tiles = count // 2
    mine = lax.rem(me, 2) == 0
    solver = me // 2

    def send(t, carry):
        @pl.when(2 * t != me)
        def _():
            remote(ends.at[t], held.at[me], sems.at[0], sems.at[1], nest, 2 * t).start()

        return carry

    lax.fori_loop(0, count, send, 0)

    @pl.when(mine)
    def _():
        pltpu.make_async_copy(ends.at[solver], held.at[me], sems.at[1]).start()
        back = solver >= tiles
        kind = jnp.where(back, solver - tiles, solver)
        ratio = jump[kind, 0]
        await_bytes(held, sems.at[1])

        def place(i):
            return jnp.where(back, group - 1 - i, i)

        def total(i, value):
            return value * ratio + held[place(i)]

        start = lax.fori_loop(0, group, total, jnp.zeros((8, LANES), f32)) * jump[kind, 1]

        def walk(i, value):
            g = place(i)
            result[g] = value

            @pl.when(g != me)
            def _():
                remote(result.at[g], dst.at[solver], sems.at[2], sems.at[3], nest, g).start()

            @pl.when(g == me)
            def _():
                pltpu.make_async_copy(result.at[g], dst.at[solver], sems.at[3]).start()

            return held[g] + ratio * value

        lax.fori_loop(0, group, walk, start)
        await_bytes(result.at[pl.ds(0, group - 1)], sems.at[2])
        await_bytes(ends.at[pl.ds(0, count - 1)], sems.at[0])

    @pl.when(jnp.logical_not(mine))
    def _():
        await_bytes(ends, sems.at[0])

    await_bytes(dst, sems.at[3])


def backward_kernel(
    coupled, spectrum, incoming, heights, back_t, modes, y_any,
    updated, pressure, y_t, waves, folded, east, sem,
):
    columns = coupled.shape[-1]
    half = columns // 2
    tiles = columns // LANES
    blocks = columns // 256
    load = pltpu.make_async_copy(y_any, y_t, sem)
    load.start()
    waves[pl.ds(8 * (ROWS + 1), 8), :] = jnp.zeros((8, columns), f32)

    def scans(t, carry):
        cols = pl.ds(pl.multiple_of(t * LANES, LANES), LANES)
        root = modes[0, :, cols]
        scale = modes[1, :, cols]
        trail = spectrum[pl.ds(8 * ROWS, 8), cols] + incoming[tiles + t]
        trails = [trail]
        for x in range(ROWS - 1, 0, -1):
            trail = spectrum[pl.ds(8 * x, 8), cols] + root * trail
            trails.append(trail)
        lead = incoming[t] + spectrum[pl.ds(0, 8), cols]
        for x in range(ROWS):
            if x:
                lead = spectrum[pl.ds(8 * x, 8), cols] + root * lead
            waves[pl.ds(8 * x, 8), cols] = (lead + root * trails[ROWS - 1 - x]) * scale
        waves[pl.ds(8 * ROWS, 8), cols] = (root * lead + trails[0]) * scale
        return carry

    lax.fori_loop(0, tiles, scans, 0)
    load.wait()
    width = min(half, 256)
    parts = []
    for part in range(2):
        high, low = split(waves[:, pl.ds(part * half, half)])
        parts.append((jnp.concatenate([high, low], axis=0), high))

    def transform(b, carry):
        cols = pl.ds(pl.multiple_of(b * width, width), width)
        values = []
        for part in range(2):
            stacked, high = parts[part]
            both = mxu(stacked, y_t[2 * part, :, cols])
            values.append((both[:EXTRA] + both[EXTRA:]) + mxu(high, y_t[2 * part + 1, :, cols]))
        folded[:, cols] = values[0] + values[1]
        folded[:, pl.ds(pl.multiple_of(half + b * width, width), width)] = values[0] - values[1]
        return carry

    lax.fori_loop(0, half // width, transform, 0)

    def turning(b, carry):
        cols = pl.ds(pl.multiple_of(b * 256, 256), 256)
        high, low = split(folded[:, cols])
        both = mxu(back_t[...], high)
        value = (both[:EXTRA] + both[EXTRA:]) + mxu(back_t[pl.ds(0, EXTRA), :], low)
        pressure[:, :, cols] = value[: ROWS * LEVELS].reshape(LEVELS, ROWS, 256)
        east[:, cols] = value[ROWS * LEVELS : ROWS * LEVELS + LEVELS]
        return carry

    lax.fori_loop(0, blocks, turning, 0)
    row = lax.broadcasted_iota(jnp.int32, (ROWS, 256), 0)

    def project(i, carry):
        z = i // blocks
        start = pl.multiple_of(lax.rem(i, blocks) * 256, 256)
        cols = pl.ds(start, 256)
        after = pl.ds(pl.multiple_of(lax.rem(start + 256, columns), LANES), LANES)
        own = pressure[z, :, cols]
        beyond = jnp.concatenate([own, pressure[z, :, after]], axis=1)
        north = pltpu.roll(beyond, 383, 1)[:, :256]
        plus = jnp.where(row == ROWS - 1, east[pl.ds(z, 1), cols], pltpu.roll(own, ROWS - 1, 0))
        top = pressure[jnp.minimum(z + 1, LEVELS - 1), :, cols]
        top = top * jnp.where(z < LEVELS - 1, 1.0, 0.0).astype(f32)
        mask = jnp.where(z >= heights[:, cols], 1.0, 0.0).astype(f32)
        updated[0, z, :, cols] = mask * (coupled[0, z, :, cols] - DT * (plus - own))
        updated[1, z, :, cols] = mask * (coupled[1, z, :, cols] - DT * (north - own))
        updated[2, z, :, cols] = mask * (coupled[2, z, :, cols] - DT * (top - own))
        return carry

    lax.fori_loop(0, LEVELS * blocks, project, 0)


def local(velocity, viscosity, heights, row_offset, column_offset):
    flow, viscous, roofs = velocity[0], viscosity[0], heights[0]
    columns = flow.shape[-1]
    group = lax.axis_size("gx")
    x_total = group * ROWS
    tiles = columns // LANES
    half = columns // 2
    t = {name: jnp.asarray(value) for name, value in tables(x_total, columns, group).items()}
    params = pltpu.CompilerParams(**PARAMS)
    effects = pltpu.CompilerParams(has_side_effects=True, **PARAMS)
    shape = lambda *dims: jax.ShapeDtypeStruct(dims, f32)
    vmem = pltpu.VMEM
    dma = pltpu.SemaphoreType.DMA

    west, east = pl.pallas_call(
        halo_kernel,
        out_shape=[shape(4, LEVELS, columns)] * 2,
        in_specs=[VMEM_SPEC] * 2,
        out_specs=[VMEM_SPEC] * 2,
        scratch_shapes=[vmem((2, 4, LEVELS, columns), f32), dma((4,))],
        compiler_params=effects,
        name="halo",
    )(flow, viscous)
    prov, chunks = pl.pallas_call(
        stencil_kernel,
        out_shape=[shape(3, LEVELS, ROWS, columns), shape(group, 3, ROWS, LANES)],
        in_specs=[SMEM_SPEC] + [VMEM_SPEC] * 6,
        out_specs=[VMEM_SPEC] * 2,
        scratch_shapes=[vmem((24 * 8, columns), f32), vmem((tiles, ROWS, LANES), f32)],
        compiler_params=params,
        name="stencil",
    )(column_offset, flow, viscous, roofs, west, east, t["pair"])
    under, above = pl.pallas_call(
        gather_kernel,
        out_shape=[shape(3, x_total + ROWS, LANES), shape(3, x_total // 2 + 3 * ROWS, LANES)],
        in_specs=[VMEM_SPEC],
        out_specs=[VMEM_SPEC] * 2,
        scratch_shapes=[dma((3,))],
        compiler_params=effects,
        name="gather",
    )(chunks)
    to_child, to_parent = pl.pallas_call(
        shift_kernel,
        out_shape=[shape(group, 32, LANES), shape(group, 48, LANES)],
        in_specs=[SMEM_SPEC] + [VMEM_SPEC] * 2,
        out_specs=[VMEM_SPEC] * 2,
        compiler_params=params,
        name="shift",
    )(row_offset, under, above)
    got = pl.pallas_call(
        scatter_kernel,
        out_shape=shape(group, 48, LANES),
        in_specs=[VMEM_SPEC] * 2,
        out_specs=VMEM_SPEC,
        scratch_shapes=[dma((3,))],
        compiler_params=effects,
        name="scatter",
    )(to_child, to_parent)
    coupled, spectrum, ends = pl.pallas_call(
        forward_kernel,
        out_shape=[shape(3, LEVELS, ROWS, columns), shape(EXTRA, columns), shape(2 * tiles, 8, LANES)],
        in_specs=[SMEM_SPEC] * 2 + [VMEM_SPEC] * 6 + [ANY_SPEC],
        out_specs=[VMEM_SPEC] * 3,
        scratch_shapes=[
            vmem((4, half, half), bf16),
            vmem((24, tiles, ROWS, LANES), f32),
            vmem((8, 32, columns), f32),
            vmem((ROWS, columns), f32),
            vmem((EXTRA, columns), f32),
            vmem((EXTRA, columns), f32),
            dma(()),
        ],
        compiler_params=params,
        name="forward",
    )(row_offset, column_offset, prov, got, roofs, t["wide"], t["turn"], t["modes"], t["y"])
    incoming = pl.pallas_call(
        chain_kernel,
        out_shape=shape(2 * tiles, 8, LANES),
        in_specs=[VMEM_SPEC] * 2,
        out_specs=VMEM_SPEC,
        scratch_shapes=[vmem((group, 8, LANES), f32), vmem((group, 8, LANES), f32), dma((4,))],
        compiler_params=effects,
        name="chain",
    )(ends, t["jump"])
    updated, pressure = pl.pallas_call(
        backward_kernel,
        out_shape=[shape(3, LEVELS, ROWS, columns), shape(LEVELS, ROWS, columns)],
        in_specs=[VMEM_SPEC] * 6 + [ANY_SPEC],
        out_specs=[VMEM_SPEC] * 2,
        scratch_shapes=[
            vmem((4, half, half), bf16),
            vmem((EXTRA, columns), f32),
            vmem((EXTRA, columns), f32),
            vmem((LEVELS, columns), f32),
            dma(()),
        ],
        compiler_params=params,
        name="backward",
    )(coupled, spectrum, incoming, roofs, t["back"], t["modes"], t["y"])
    return updated[None], pressure[None]


def solution(mesh):
    return jax.shard_map(
        local,
        mesh=mesh,
        in_specs=(
            P("nest", None, None, "gx", None),
            P("nest", None, "gx", None),
            P("nest", "gx", None),
            P(),
            P(),
        ),
        out_specs=(P("nest", None, None, "gx", None), P("nest", None, "gx", None)),
        check_vma=False,
    )
```

time: 664 us -> 220 us (0.33); the launches traced: 655 us -> 219 us
  Pallas kernels: 0 us -> 214 us
  local copies, waits for them, and re-layouts: 201 us -> 3.58 us
  matrix products: 176 us -> 0 us
  other arithmetic: 143 us -> 0 us
  waiting for transfers between devices: 82.9 us -> 0 us
  starting transfers between devices: 49.2 us -> 0 us
    pallas_call x0 -> x8, Pallas kernels: none -> 214 us  [the longest x1 45.4 us: local(): pl.pallas_call(gather_kernel, out_shape=[shape(3, x_total + ROWS, LANES),...]
    dot_general x6 -> x0, matrix products: 176 us -> none  [the longest x1 76.4 us: local(): jnp.dot(source.reshape(levels * row_count, columns), table_y, precision=h...]
    dot_general x3 -> x0, other arithmetic: 85.3 us -> none  [the longest x1 67.1 us: local(): jnp.dot(lax.all_to_all(physical, 'gx', split_axis=1, concat_axis=2, tiled...]
    all_to_all x8 -> x0, local copies, waits for them, and re-layouts: 82.9 us -> none  [the longest x4 41 us: local(): lax.all_to_all(outgoing, 'gx', split_axis=3, concat_axis=1, tiled=True)]
    unnamed x28 -> x20, local copies, waits for them, and re-layouts: 55.3 us -> 3.58 us
    all_to_all x4 -> x0, waiting for transfers between devices: 44.7 us -> none  [the longest x1 22.5 us: local(): lax.all_to_all(received, 'gx', split_axis=1, concat_axis=3, tiled=True)]
    ppermute x5 -> x0, waiting for transfers between devices: 38.2 us -> none  [the longest x1 33.9 us: swapped(): return lax.ppermute(value, axis, pairs)]
    all_to_all x4 -> x0, starting transfers between devices: 36.2 us -> none  [the longest x1 11.4 us: local(): lax.all_to_all(flat.reshape(levels, row_count, columns), 'gx', split_axis...]
  transfers between devices with their start and end apart: 9 -> 0, of which waited for: 5 -> 0; matrix products, arithmetic and copies ran while one was open for 15% -> 0% of each run, Pallas kernels for 0% -> 0%
where the time goes in v1:
time: 220 us; the launch traced here: 219 us
  Pallas kernels  214 us (97%)
  local copies, waits for them, and re-layouts  3.58 us (2%)
    pallas_call x1, Pallas kernels, local(): pl.pallas_call(gather_kernel, out_shape=[shape(3, x_total + ROWS, LANES),...  45.4 us
    pallas_call x1, Pallas kernels, local(): pl.pallas_call(forward_kernel, out_shape=[shape(3, LEVELS, ROWS, columns)...  44 us
    pallas_call x1, Pallas kernels, local(): pl.pallas_call(scatter_kernel, out_shape=shape(group, 48, LANES), in_spec...  37.9 us
    pallas_call x1, Pallas kernels, local(): pl.pallas_call(stencil_kernel, out_shape=[shape(3, LEVELS, ROWS, columns)...  26 us
    pallas_call x1, Pallas kernels, local(): pl.pallas_call(chain_kernel, out_shape=shape(2 * tiles, 8, LANES), in_spe...  21.4 us
    pallas_call x1, Pallas kernels, local(): pl.pallas_call(halo_kernel, out_shape=[shape(4, LEVELS, columns)] * 2, in...  18.5 us
    pallas_call x1, Pallas kernels, local(): pl.pallas_call(backward_kernel, out_shape=[shape(3, LEVELS, ROWS, columns...  17.1 us

profile of v1, /device:TPU:1, one launch (start us, length us, event | category | flops | bytes accessed | tf_op | source)
XLA Modules:
  0.0 219.4 jit_solution(18170829550199871672)
XLA Ops:
  1.9 0.0 copy-start
  1.9 1.2 copy-done
  3.1 0.0 copy-start.3
  3.2 0.0 copy-start.9
  3.2 18.5 %halo.1 = (f32[4,8,2048]{2,1,0:T(8,128)S(1)}, f32[4,8,2048]{2,1,0:T(8,128)S(1)}) custom-call(f32[3,8,16,2048]{3,2,1,0:T(8,128)} %bitcast.10, f32[8,16,2048]{2,1,0:T(8,128)S(1)} %bitcast.5), custom_call_target="tpu_custom_call" | custom-call | tf_op jit(solution)/shard_map/halo/pallas_call | solution.py:642
  21.6 0.0 copy-done.3
  21.7 0.0 copy-done.9
  21.7 26.0 %stencil.1 = (f32[3,8,16,2048]{3,2,1,0:T(8,128)}, f32[64,3,16,128]{3,2,1,0:T(8,128)S(1)}) custom-call(s32[1]{0:T(128)S(6)} %copy.15.oy_ref, f32[3,8,16,2048]{3,2,1,0:T(8,128)} %bitcast.11, f32[8,16,2048]{2,1,0:T(8,128)S(1)} %bitcast.6, s32[16,2048]{1,0:T(8,128)S(1)} %bitcast.7, f32[4,8,2048]{2,1,0:T(8,128)S(1)} %get-tuple-element.15.west, ...), custom_call_target="tpu_custom_call" | custom-call | tf_op jit(solution)/shard_map/stencil/pallas_call | solution.py:651
  47.7 45.4 %gather.1 = (f32[3,1040,128]{2,1,0:T(8,128)S(1)}, f32[3,560,128]{2,1,0:T(8,128)S(1)}) custom-call(f32[64,3,16,128]{3,2,1,0:T(8,128)S(1)} %get-tuple-element.18.src), custom_call_target="tpu_custom_call" | custom-call | tf_op jit(solution)/shard_map/gather/pallas_call | solution.py:660
  93.1 0.0 copy-start.1
  93.1 1.2 copy-done.1
  94.3 0.0 copy-start.4
  94.3 0.0 copy-start.5
  94.3 0.0 copy-start.7
  94.3 3.4 %shift.1 = (f32[64,32,128]{2,1,0:T(8,128)S(1)}, f32[64,48,128]{2,1,0:T(8,128)S(1)}) custom-call(s32[1]{0:T(128)S(6)} %copy.14.ox_ref, f32[3,1040,128]{2,1,0:T(8,128)} %copy-done.1, f32[3,560,128]{2,1,0:T(8,128)S(1)} %get-tuple-element.20.above), custom_call_target="tpu_custom_call" | custom-call | tf_op jit(solution)/shard_map/shift/pallas_call | solution.py:669
  97.7 0.0 copy-start.2
  97.7 1.2 copy-done.2
  98.8 37.9 %scatter.1.got = f32[64,48,128]{2,1,0:T(8,128)S(1)} custom-call(f32[64,32,128]{2,1,0:T(8,128)S(1)} %get-tuple-element.21.to_child, f32[64,48,128]{2,1,0:T(8,128)} %copy-done.2), custom_call_target="tpu_custom_call" | custom-call | tf_op jit(solution)/shard_map/scatter/pallas_call | solution.py:677
  136.7 0.0 copy-done.4
  136.7 0.0 copy-done.5
  136.7 0.0 copy-done.7
  136.8 0.0 copy-start.8
  136.8 0.0 copy-start.6
  136.8 44.0 %forward.1 = (f32[3,8,16,2048]{3,2,1,0:T(8,128)}, f32[144,2048]{1,0:T(8,128)S(1)}, f32[32,8,128]{2,1,0:T(8,128)S(1)}) custom-call(s32[1]{0:T(128)S(6)} %copy.14.ox_ref, s32[1]{0:T(128)S(6)} %copy.15.oy_ref, f32[3,8,16,2048]{3,2,1,0:T(8,128)} %get-tuple-element.17.prov, f32[64,48,128]{2,1,0:T(8,128)S(1)} %scatter.1.got, s32[16,2048]{1,0:T(8,128)S(1)} %bitcast.8, ...), custom_call_target="tpu_custom_call" | custom-call | tf_op jit(solution)/shard_map/forward/pallas_call | solution.py:686
  180.8 0.0 copy-done.8
  180.8 21.4 %chain.1.incoming = f32[32,8,128]{2,1,0:T(8,128)S(1)} custom-call(f32[32,8,128]{2,1,0:T(8,128)S(1)} %get-tuple-element.25.ends, f32[16,2,8,128]{3,2,1,0:T(8,128)S(1)} %copy-done.8), custom_call_target="tpu_custom_call" | custom-call | tf_op jit(solution)/shard_map/chain/pallas_call | solution.py:703
  202.2 0.0 copy-done.6
  202.2 17.1 %backward.1 = (f32[3,8,16,2048]{3,2,1,0:T(8,128)}, f32[8,16,2048]{2,1,0:T(8,128)}) custom-call(f32[3,8,16,2048]{3,2,1,0:T(8,128)} %get-tuple-element.23.coupled, f32[144,2048]{1,0:T(8,128)S(1)} %get-tuple-element.24.spectrum, f32[32,8,128]{2,1,0:T(8,128)S(1)} %chain.1.incoming, s32[16,2048]{1,0:T(8,128)S(1)} %bitcast.9, bf16[288,144]{1,0:T(8,128)(2,1)S(1)} %copy-done.6, ...), custom_call_target="tpu_custom_call" | custom-call | tf_op jit(solution)/shard_map/backward/pallas_call | solution.py:712
Async XLA Ops:
  1.9 1.2 copy-start
  3.1 18.5 %copy-start.3 = (s32[1,16,2048]{2,1,0:T(8,128)S(1)}, s32[1,16,2048]{2,1,0:T(8,128)}, u32[]{:S(2)}) copy-start(s32[1,16,2048]{2,1,0:T(8,128)} %param.14) | copy-start | bytes 393220
  3.2 18.5 %copy-start.9 = (bf16[256,128]{1,0:T(8,128)(2,1)S(1)}, bf16[256,128]{1,0:T(8,128)(2,1)}, u32[]{:S(2)}) copy-start(bf16[256,128]{1,0:T(8,128)(2,1)} %constant.20.clone.pair) | copy-start | bytes 196612
  93.1 1.2 copy-start.1
  94.3 42.4 %copy-start.4 = (f32[2,8,2048]{2,1,0:T(8,128)S(1)}, f32[2,8,2048]{2,1,0:T(8,128)}, u32[]{:S(2)}) copy-start(f32[2,8,2048]{2,1,0:T(8,128)} %constant.17.clone.modes) | copy-start | bytes 393220
  94.3 42.5 %copy-start.5 = (bf16[2,256,256]{2,1,0:T(8,128)(2,1)S(1)}, bf16[2,256,256]{2,1,0:T(8,128)(2,1)}, u32[]{:S(2)}) copy-start(bf16[2,256,256]{2,1,0:T(8,128)(2,1)} %constant.19.clone.wide_t) | copy-start | bytes 786436
  94.3 42.5 %copy-start.7 = (bf16[288,144]{1,0:T(8,128)(2,1)S(1)}, bf16[288,144]{1,0:T(8,128)(2,1)}, u32[]{:S(2)}) copy-start(bf16[288,144]{1,0:T(8,128)(2,1)} %constant.15.clone.turn_t) | copy-start | bytes 248836
  97.7 1.2 copy-start.2
  136.8 44.0 %copy-start.8 = (f32[16,2,8,128]{3,2,1,0:T(8,128)S(1)}, f32[16,2,8,128]{3,2,1,0:T(8,128)}, u32[]{:S(2)}) copy-start(f32[16,2,8,128]{3,2,1,0:T(8,128)} %constant.18.clone.jump) | copy-start | bytes 393220
  136.8 65.5 %copy-start.6 = (bf16[288,144]{1,0:T(8,128)(2,1)S(1)}, bf16[288,144]{1,0:T(8,128)(2,1)}, u32[]{:S(2)}) copy-start(bf16[288,144]{1,0:T(8,128)(2,1)} %constant.16.clone.back_t) | copy-start | bytes 248836

commit v2 on v1

--- a/solution.py
+++ b/solution.py
@@ -96,16 +96,27 @@
     return jnp.dot(left, right, preferred_element_type=f32)
 
 
+def greet(nest, k):
+    pl.semaphore_signal(
+        pltpu.get_barrier_semaphore(), inc=1, device_id={"nest": nest, "gx": k},
+        device_id_type=pl.DeviceIdType.MESH,
+    )
+
+
 def halo_kernel(vel, visc, west, east, edge, sems):
     me = lax.axis_index("gx")
+    nest = lax.axis_index("nest")
     group = lax.axis_size("gx")
+    right = lax.rem(me + 1, group)
+    left = lax.rem(me + group - 1, group)
+    greet(nest, left)
+    greet(nest, right)
     for c in range(3):
         edge[0, c] = vel[c, :, 0, :]
         edge[1, c] = vel[c, :, ROWS - 1, :]
     edge[0, 3] = visc[:, 0, :]
     edge[1, 3] = visc[:, ROWS - 1, :]
-    right = lax.rem(me + 1, group)
-    left = lax.rem(me + group - 1, group)
+    pl.semaphore_wait(pltpu.get_barrier_semaphore(), 2)
     to_right = pltpu.make_async_remote_copy(
         edge.at[1], west, sems.at[0], sems.at[1], device_id={"gx": right},
         device_id_type=pl.DeviceIdType.MESH,
@@ -183,19 +194,18 @@
         shift = lax.rem(oy, LANES)
         turn = lax.rem(LANES - shift, LANES)
 
-        def unit(i, carry):
-            cz = i // blocks
-            b = lax.rem(i, blocks)
+        def unit(cz, carry):
             c = cz // LEVELS
             z = lax.rem(cz, LEVELS)
-            one = pl.ds(pl.multiple_of(lax.rem(first + b, tiles) * LANES, LANES), LANES)
-            two = pl.ds(pl.multiple_of(lax.rem(first + b + 1, tiles) * LANES, LANES), LANES)
-            low = pltpu.roll(prov[c, z, :, one], turn, 1)
-            high = pltpu.roll(prov[c, z, :, two], turn, 1)
-            out[b * 8 + cz // 3, lax.rem(cz, 3)] = jnp.where(lane < LANES - shift, low, high)
-            return carry
-
-        lax.fori_loop(0, 24 * blocks, unit, 0)
+            moved = []
+            for b in range(blocks + 1):
+                cols = pl.ds(pl.multiple_of(lax.rem(first + b, tiles) * LANES, LANES), LANES)
+                moved.append(pltpu.roll(prov[c, z, :, cols], turn, 1))
+            for b in range(blocks):
+                out[cz, :, pl.ds(b * LANES, LANES)] = jnp.where(lane < LANES - shift, moved[b], moved[b + 1])
+            return carry
+
+        lax.fori_loop(0, 24, unit, 0)
 
     @pl.when(is_child)
     def _():
@@ -214,7 +224,7 @@
         for b in range(blocks):
             high, low = split(mean[:, pl.ds(b * 256, 256)])
             value = mxu(high, pair[...]) + mxu(low, pair[...])
-            out[pl.ds(b * 8, 8), :, pl.ds(0, 8), :] = value.reshape(8, 3, 8, LANES)
+            out[:, pl.ds(0, 8), pl.ds(b * LANES, LANES)] = value.reshape(24, 8, LANES)
 
 
 def remote(src, dst, send, recv, nest, k):
@@ -228,101 +238,85 @@
     pltpu.make_async_copy(ref, ref, sem).wait()
 
 
-def gather_kernel(src, under, above, sems):
-    group = src.shape[0]
-    x_total = group * ROWS
-    half = x_total // 2
+def align_kernel(src, beside, sems):
     me = lax.axis_index("gx")
     nest = lax.axis_index("nest")
-    here = pl.ds(pl.multiple_of(me * ROWS, ROWS), ROWS)
-
-    @pl.when(nest == 0)
-    def _():
-        def send_rows(i, carry):
-            k = lax.rem(me + i, group)
-            remote(src.at[k], under.at[:, here], sems.at[0], sems.at[1], 0, k).start()
-            return carry
-
-        lax.fori_loop(1, group, send_rows, 0)
-        pltpu.make_async_copy(src.at[me], under.at[:, here], sems.at[1]).start()
-        blank = jnp.zeros((3, ROWS, LANES), f32)
-        under[:, pl.ds(x_total, ROWS)] = blank
-        above[:, pl.ds(0, ROWS)] = blank
-        above[:, pl.ds(ROWS + half, ROWS)] = blank
-        above[:, pl.ds(2 * ROWS + half, ROWS)] = blank
-        await_bytes(src.at[pl.ds(0, group - 1)], sems.at[0])
-        await_bytes(under.at[:, pl.ds(0, x_total)], sems.at[1])
-        await_bytes(above.at[:, pl.ds(ROWS, half)], sems.at[2])
-
-    @pl.when(nest == 1)
-    def _():
-        slot = pl.ds(pl.multiple_of(ROWS + me * 8, 8), 8)
-
-        def send_means(i, carry):
-            k = lax.rem(me + i, group)
-            remote(src.at[k, :, pl.ds(0, 8)], above.at[:, slot], sems.at[0], sems.at[2], 0, k).start()
-            return carry
-
-        lax.fori_loop(0, group, send_means, 0)
-        await_bytes(src.at[:, :, pl.ds(0, 8)], sems.at[0])
-
-
-def shift_kernel(ox_ref, under, above, to_child, to_parent):
-    group = to_child.shape[0]
-    half = group * ROWS // 2
+    group = lax.axis_size("gx")
+    step = jnp.where(nest == 0, group - 1, 1)
+    target = lax.rem(me + step, group)
+    greet(nest, lax.rem(me + group - step, group))
+    pl.semaphore_wait(pltpu.get_barrier_semaphore(), 1)
+    copy = remote(src.at[:, pl.ds(0, 8)], beside, sems.at[0], sems.at[1], nest, target)
+    copy.start()
+    copy.wait()
+
+
+def shift_kernel(ox_ref, own, beside, even, odd):
+    group = lax.axis_size("gx")
+    half = own.shape[-1]
+    me = lax.axis_index("gx")
+    ox = ox_ref[0]
+    rest = lax.rem(ox, 8)
+    parity = lax.rem(ox // 8 + me, 2)
 
     @pl.when(lax.axis_index("nest") == 0)
     def _():
-        ox = ox_ref[0]
-
-        def fill(g, carry):
-            rows = pl.ds(pl.multiple_of((ox // 8 + g) * 8, 8), 16)
-            first = jnp.clip(ROWS * g - ox + ROWS, 0, half + ROWS)
-            back = pl.ds(pl.multiple_of(first // 8 * 8, 8), 24)
-            for u in range(3):
-                moved = pltpu.roll(under[u, rows], lax.rem(16 - lax.rem(ox, 8), 16), 0)
-                to_child[g, pl.ds(u * 9, 9)] = moved[:9]
-                moved = pltpu.roll(above[u, back], lax.rem(24 - lax.rem(first, 8), 24), 0)
-                to_parent[g, pl.ds(u * ROWS, ROWS)] = moved[:ROWS]
-            return carry
-
-        lax.fori_loop(0, group, fill, 0)
-
-
-def scatter_kernel(to_child, to_parent, dst, sems):
-    group = to_child.shape[0]
-    me = lax.axis_index("gx")
-    nest = lax.axis_index("nest")
-
-    @pl.when(nest == 0)
-    def _():
-        def send(i, carry):
-            k = lax.rem(me + i, group)
-            remote(to_child.at[k], dst.at[me, pl.ds(0, 32)], sems.at[0], sems.at[1], 1, k).start()
-
-            @pl.when(i > 0)
-            def _():
-                remote(to_parent.at[k], dst.at[me], sems.at[2], sems.at[1], 0, k).start()
-
-            return carry
-
-        lax.fori_loop(0, group, send, 0)
-        pltpu.make_async_copy(to_parent.at[me], dst.at[me], sems.at[1]).start()
-        await_bytes(to_child, sems.at[0])
-        await_bytes(to_parent.at[pl.ds(0, group - 1)], sems.at[2])
-        await_bytes(dst, sems.at[1])
-
-    @pl.when(nest == 1)
-    def _():
-        await_bytes(dst.at[:, pl.ds(0, 32)], sems.at[1])
+        def fill(i, carry):
+            for b in range(half // LANES):
+                cols = pl.ds(b * LANES, LANES)
+                ninths = ([], [])
+                for j in range(8):
+                    cz = i * 8 + j
+                    rows = jnp.concatenate([own[cz, :, cols], beside[cz, :, cols]], axis=0)
+                    rows = pltpu.roll(rows, lax.rem(24 - rest, 24), 0)
+                    place = pl.ds(pl.multiple_of(cz * 8, 8), 8)
+                    even[place, cols] = rows[:8]
+                    odd[place, cols] = rows[8:16]
+                    ninths[0].append(rows[8:9])
+                    ninths[1].append(rows[16:17])
+                place = pl.ds(pl.multiple_of(192 + i * 8, 8), 8)
+                even[place, cols] = jnp.concatenate(ninths[0], axis=0)
+                odd[place, cols] = jnp.concatenate(ninths[1], axis=0)
+            return carry
+
+        lax.fori_loop(0, 3, fill, 0)
+
+    @pl.when(lax.axis_index("nest") == 1)
+    def _():
+        mine = jnp.full((8, LANES), parity, jnp.int32) == 0
+
+        def fill(cz, carry):
+            place = pl.ds(pl.multiple_of(cz * 8, 8), 8)
+            for b in range(half // LANES):
+                cols = pl.ds(b * LANES, LANES)
+                value = own[cz, pl.ds(0, 8), cols]
+                rows = jnp.concatenate([value, beside[cz, :, cols]], axis=0)
+                rows = pltpu.roll(rows, rest, 0)
+                even[place, cols] = jnp.where(mine, rows[:8], rows[8:])
+                odd[place, cols] = jnp.where(mine, rows[8:], rows[:8])
+            return carry
+
+        lax.fori_loop(0, 24, fill, 0)
+
+
+def cross(shift, group, even, odd):
+    pairs = ([], [])
+    for g in range(group):
+        block = shift + g
+        pairs[block % 2].append((block // 2, group + g))
+        pairs[block % 2].append((group + g, block // 2))
+    if shift < group:
+        pairs[shift % 2].append((2 * group - 1, (shift + group) // 2))
+    axes = ("nest", "gx")
+    return lax.ppermute(even, axes, pairs[0]), lax.ppermute(odd, axes, pairs[1])
 
 
 def forward_kernel(
-    ox_ref, oy_ref, prov, got, heights, wide_t, turn_t, modes, y_any,
+    ox_ref, oy_ref, prov, even, odd, heights, wide_t, turn_t, modes, y_any,
     coupled, spectrum, ends, y_t, mapped, wide, rate, source, turned, sem,
 ):
     columns = prov.shape[-1]
-    group = got.shape[0]
+    group = lax.axis_size("gx")
     x_total = group * ROWS
     half = columns // 2
     tiles = columns // LANES
@@ -338,29 +332,36 @@
 
     @pl.when(is_child)
     def _():
+        first_is_even = jnp.full((216, LANES), lax.rem(ox // 8 + me, 2), jnp.int32) == 0
+
+        def block(b):
+            cols = pl.ds(b * LANES, LANES)
+            return jnp.where(first_is_even, even[:, cols], odd[:, cols])
+
+        left = block(0)
         for b in range(blocks):
-            left = got[pl.ds(b * 8, 8), pl.ds(0, 32), :].reshape(256, LANES)
-            nxt = min(b + 1, blocks - 1)
-            right = got[pl.ds(nxt * 8, 8), pl.ds(0, 32), :].reshape(256, LANES)
+            right = block(min(b + 1, blocks - 1))
             high, low = split(jnp.concatenate([left, right], axis=1))
             table = wide_t[0 if b < blocks - 1 else 1]
-            wide[:, :, pl.ds(b * 256, 256)] = (mxu(high, table) + mxu(low, table)).reshape(8, 32, 256)
-        last = me == group - 1
-
-        def unit(kz, carry):
-            for u in range(3):
-                cz = kz * 3 + u
-                for t in range(tiles):
-                    cols = pl.ds(t * LANES, LANES)
-                    own = wide[kz, pl.ds(u * 9, 8), cols]
-                    after = wide[kz, pl.ds(u * 9 + 1, 8), cols]
-                    tail = lax.broadcasted_iota(jnp.int32, (8, LANES), 0) == 7
-                    after = jnp.where(jnp.logical_and(tail, last), own, after)
+            wide[:, pl.ds(b * 256, 256)] = mxu(high, table) + mxu(low, table)
+            left = right
+        tail = lax.broadcasted_iota(jnp.int32, (8, LANES), 0) == 7
+        last = jnp.full((8, LANES), me, jnp.int32) == group - 1
+
+        def unit(i, carry):
+            for t in range(tiles):
+                cols = pl.ds(t * LANES, LANES)
+                ninths = wide[pl.ds(pl.multiple_of(192 + i * 8, 8), 8), cols]
+                for j in range(8):
+                    cz = i * 8 + j
+                    own = wide[pl.ds(pl.multiple_of(cz * 8, 8), 8), cols]
+                    ninth = jnp.where(last, own, ninths[j : j + 1])
+                    after = jnp.where(tail, ninth, pltpu.roll(own, 7, 0))
                     mapped[cz, t, pl.ds(0, 8, stride=2), :] = own
                     mapped[cz, t, pl.ds(1, 8, stride=2), :] = 0.5 * (own + after)
             return carry
 
-        lax.fori_loop(0, 8, unit, 0)
+        lax.fori_loop(0, 3, unit, 0)
 
         def rates(t, carry):
             cols = pl.ds(pl.multiple_of(t * LANES, LANES), LANES)
@@ -379,20 +380,20 @@
         first = oy // LANES
         shift = lax.rem(oy, LANES)
 
-        def unit(i, carry):
-            cz = i // tiles
-            t = lax.rem(i, tiles)
-            at = lax.rem(t - first + tiles, tiles)
-            low = jnp.minimum(at, blocks - 1)
-            high = jnp.minimum(lax.rem(at + tiles - 1, tiles), blocks - 1)
-            kz = cz // 3
-            rows = pl.ds(pl.multiple_of(lax.rem(cz, 3) * ROWS, ROWS), ROWS)
-            one = pltpu.roll(got[low * 8 + kz, rows, :], shift, 1)
-            two = pltpu.roll(got[high * 8 + kz, rows, :], shift, 1)
-            mapped[cz, t] = jnp.where(lane >= shift, one, two)
-            return carry
-
-        lax.fori_loop(0, 24 * tiles, unit, 0)
+        def unit(cz, carry):
+            rows = pl.ds(pl.multiple_of(cz * 8, 8), 8)
+            moved = []
+            for b in range(blocks):
+                cols = pl.ds(b * LANES, LANES)
+                both = jnp.concatenate([even[rows, cols], odd[rows, cols]], axis=0)
+                moved.append(pltpu.roll(both, shift, 1))
+            for b in range(blocks + 1):
+                own = moved[min(b, blocks - 1)]
+                before = moved[max(b - 1, 0)]
+                mapped[cz, lax.rem(first + b, tiles)] = jnp.where(lane >= shift, own, before)
+            return carry
+
+        lax.fori_loop(0, 24, unit, 0)
 
         def rates(t, carry):
             cols = pl.ds(pl.multiple_of(t * LANES, LANES), LANES)
@@ -493,6 +494,24 @@
     mine = lax.rem(me, 2) == 0
     solver = me // 2
 
+    @pl.when(mine)
+    def _():
+        def hello(i, carry):
+            greet(nest, lax.rem(me + i, group))
+            return carry
+
+        lax.fori_loop(1, group, hello, 0)
+        pl.semaphore_wait(pltpu.get_barrier_semaphore(), group - 1)
+
+    @pl.when(jnp.logical_not(mine))
+    def _():
+        def hello(i, carry):
+            greet(nest, 2 * i)
+            return carry
+
+        lax.fori_loop(0, count, hello, 0)
+        pl.semaphore_wait(pltpu.get_barrier_semaphore(), count)
+
     def send(t, carry):
         @pl.when(2 * t != me)
         def _():
@@ -634,7 +653,7 @@
     half = columns // 2
     t = {name: jnp.asarray(value) for name, value in tables(x_total, columns, group).items()}
     params = pltpu.CompilerParams(**PARAMS)
-    effects = pltpu.CompilerParams(has_side_effects=True, **PARAMS)
+    effects = lambda number: pltpu.CompilerParams(has_side_effects=True, collective_id=number, **PARAMS)
     shape = lambda *dims: jax.ShapeDtypeStruct(dims, f32)
     vmem = pltpu.VMEM
     dma = pltpu.SemaphoreType.DMA
@@ -645,53 +664,50 @@
         in_specs=[VMEM_SPEC] * 2,
         out_specs=[VMEM_SPEC] * 2,
         scratch_shapes=[vmem((2, 4, LEVELS, columns), f32), dma((4,))],
-        compiler_params=effects,
+        compiler_params=effects(0),
         name="halo",
     )(flow, viscous)
     prov, chunks = pl.pallas_call(
         stencil_kernel,
-        out_shape=[shape(3, LEVELS, ROWS, columns), shape(group, 3, ROWS, LANES)],
+        out_shape=[shape(3, LEVELS, ROWS, columns), shape(24, ROWS, half)],
         in_specs=[SMEM_SPEC] + [VMEM_SPEC] * 6,
         out_specs=[VMEM_SPEC] * 2,
         scratch_shapes=[vmem((24 * 8, columns), f32), vmem((tiles, ROWS, LANES), f32)],
         compiler_params=params,
         name="stencil",
     )(column_offset, flow, viscous, roofs, west, east, t["pair"])
-    under, above = pl.pallas_call(
-        gather_kernel,
-        out_shape=[shape(3, x_total + ROWS, LANES), shape(3, x_total // 2 + 3 * ROWS, LANES)],
+    beside = pl.pallas_call(
+        align_kernel,
+        out_shape=shape(24, 8, half),
         in_specs=[VMEM_SPEC],
-        out_specs=[VMEM_SPEC] * 2,
-        scratch_shapes=[dma((3,))],
-        compiler_params=effects,
-        name="gather",
+        out_specs=VMEM_SPEC,
+        scratch_shapes=[dma((2,))],
+        compiler_params=effects(1),
+        name="align",
     )(chunks)
-    to_child, to_parent = pl.pallas_call(
+    even, odd = pl.pallas_call(
         shift_kernel,
-        out_shape=[shape(group, 32, LANES), shape(group, 48, LANES)],
+        out_shape=[shape(216, half)] * 2,
         in_specs=[SMEM_SPEC] + [VMEM_SPEC] * 2,
         out_specs=[VMEM_SPEC] * 2,
         compiler_params=params,
         name="shift",
-    )(row_offset, under, above)
-    got = pl.pallas_call(
-        scatter_kernel,
-        out_shape=shape(group, 48, LANES),
-        in_specs=[VMEM_SPEC] * 2,
-        out_specs=VMEM_SPEC,
-        scratch_shapes=[dma((3,))],
-        compiler_params=effects,
-        name="scatter",
-    )(to_child, to_parent)
+    )(row_offset, chunks, beside)
+    even, odd = lax.switch(
+        row_offset[0] // 8,
+        [functools.partial(cross, number, group) for number in range(group + 1)],
+        even,
+        odd,
+    )
     coupled, spectrum, ends = pl.pallas_call(
         forward_kernel,
         out_shape=[shape(3, LEVELS, ROWS, columns), shape(EXTRA, columns), shape(2 * tiles, 8, LANES)],
-        in_specs=[SMEM_SPEC] * 2 + [VMEM_SPEC] * 6 + [ANY_SPEC],
+        in_specs=[SMEM_SPEC] * 2 + [VMEM_SPEC] * 7 + [ANY_SPEC],
         out_specs=[VMEM_SPEC] * 3,
         scratch_shapes=[
             vmem((4, half, half), bf16),
             vmem((24, tiles, ROWS, LANES), f32),
-            vmem((8, 32, columns), f32),
+            vmem((216, columns), f32),
             vmem((ROWS, columns), f32),
             vmem((EXTRA, columns), f32),
             vmem((EXTRA, columns), f32),
@@ -699,14 +715,14 @@
         ],
         compiler_params=params,
         name="forward",
-    )(row_offset, column_offset, prov, got, roofs, t["wide"], t["turn"], t["modes"], t["y"])
+    )(row_offset, column_offset, prov, even, odd, roofs, t["wide"], t["turn"], t["modes"], t["y"])
     incoming = pl.pallas_call(
         chain_kernel,
         out_shape=shape(2 * tiles, 8, LANES),
         in_specs=[VMEM_SPEC] * 2,
         out_specs=VMEM_SPEC,
         scratch_shapes=[vmem((group, 8, LANES), f32), vmem((group, 8, LANES), f32), dma((4,))],
-        compiler_params=effects,
+        compiler_params=effects(2),
         name="chain",
     )(ends, t["jump"])
     updated, pressure = pl.pallas_call(

time: 220 us -> 195 us (0.89)
  Pallas kernels: 214 us -> 177 us
  starting transfers between devices: 0 us -> 14.2 us
  local copies, waits for them, and re-layouts: 3.58 us -> 1.25 us
    pallas_call x3 -> x2, Pallas kernels: 86.7 us -> 21.4 us  [the longest x1 20.9 us: local(): pl.pallas_call(align_kernel, out_shape=shape(24, 8, half), in_specs=[VMEM...]
    pallas_call x1, Pallas kernels: 21.4 us -> 85.1 us  [local(): pl.pallas_call(chain_kernel, out_shape=shape(2 * tiles, 8, LANES), in_spe...]
    pallas_call x1, Pallas kernels: 44 us -> 18.7 us  [local(): pl.pallas_call(forward_kernel, out_shape=[shape(3, LEVELS, ROWS, columns)...]
    ppermute x0 -> x2, starting transfers between devices: none -> 14.2 us  [the longest x1 12.6 us: cross(): lax.ppermute(even, axes, pairs[0])]
    pallas_call x1, Pallas kernels: 26 us -> 14 us  [local(): pl.pallas_call(stencil_kernel, out_shape=[shape(3, LEVELS, ROWS, columns)...]
    unnamed x20 -> x16, local copies, waits for them, and re-layouts: 3.58 us -> 1.25 us
  transfers between devices with their start and end apart: 0 -> 2, of which waited for: 0 -> 0; matrix products, arithmetic and copies ran while one was open for 0% -> 0% of each run, Pallas kernels for 0% -> 0%
where the time goes in v2:
time: 195 us; the launch traced here: 194 us
  Pallas kernels  177 us (91%)
  starting transfers between devices  14.2 us (7%)
  between operations  2.23 us (1%)
    pallas_call x1, Pallas kernels, local(): pl.pallas_call(chain_kernel, out_shape=shape(2 * tiles, 8, LANES), in_spe...  85.1 us
    pallas_call x1, Pallas kernels, local(): pl.pallas_call(align_kernel, out_shape=shape(24, 8, half), in_specs=[VMEM...  20.9 us
    pallas_call x1, Pallas kernels, local(): pl.pallas_call(halo_kernel, out_shape=[shape(4, LEVELS, columns)] * 2, in...  20.4 us
    pallas_call x1, Pallas kernels, local(): pl.pallas_call(forward_kernel, out_shape=[shape(3, LEVELS, ROWS, columns)...  18.7 us
    pallas_call x1, Pallas kernels, local(): pl.pallas_call(backward_kernel, out_shape=[shape(3, LEVELS, ROWS, columns...  17.2 us
    pallas_call x1, Pallas kernels, local(): pl.pallas_call(stencil_kernel, out_shape=[shape(3, LEVELS, ROWS, columns)...  14 us
    ppermute x1, starting transfers between devices, cross(): lax.ppermute(even, axes, pairs[0])  12.6 us
  transfers between devices with their start and end apart: 2, of which 0 were waited for; matrix products, arithmetic and copies ran while one was open for 0% of the time, Pallas kernels for 0%

profile of v2, /device:TPU:1, one launch (start us, length us, event | category | flops | bytes accessed | tf_op | source)
XLA Modules:
  0.0 194.4 jit_solution(7027393716342560045)
XLA Ops:
  1.9 0.0 copy-start
  2.0 1.2 copy-done
  3.2 0.0 copy-start.1
  3.2 0.0 copy-start.7
  3.2 20.4 %halo.1 = (f32[4,8,2048]{2,1,0:T(8,128)S(1)}, f32[4,8,2048]{2,1,0:T(8,128)S(1)}) custom-call(f32[3,8,16,2048]{3,2,1,0:T(8,128)} %bitcast.15, f32[8,16,2048]{2,1,0:T(8,128)S(1)} %bitcast.10), custom_call_target="tpu_custom_call" | custom-call | tf_op jit(solution)/shard_map/halo/pallas_call | solution.py:661
  23.5 0.0 copy-done.1
  23.6 0.0 copy-done.7
  23.6 14.0 %stencil.1 = (f32[3,8,16,2048]{3,2,1,0:T(8,128)}, f32[24,16,1024]{2,1,0:T(8,128)S(1)}) custom-call(s32[1]{0:T(128)S(6)} %copy.145.oy_ref, f32[3,8,16,2048]{3,2,1,0:T(8,128)} %bitcast.16, f32[8,16,2048]{2,1,0:T(8,128)S(1)} %bitcast.11, s32[16,2048]{1,0:T(8,128)S(1)} %bitcast.12, f32[4,8,2048]{2,1,0:T(8,128)S(1)} %get-tuple-element.403.west, ...), custom_call_target="tpu_custom_call" | custom-call | tf_op jit(solution)/shard_map/stencil/pallas_call | solution.py:670
  37.6 0.0 copy-start.2
  37.6 0.0 copy-start.3
  37.6 0.0 copy-start.5
  37.6 20.9 %align.1.beside = f32[24,8,1024]{2,1,0:T(8,128)S(1)} custom-call(f32[24,16,1024]{2,1,0:T(8,128)S(1)} %get-tuple-element.406.src.own), custom_call_target="tpu_custom_call" | custom-call | tf_op jit(solution)/shard_map/align/pallas_call | solution.py:679
  58.5 0.5 shift.1
  59.0 14.2 %conditional.1 = (f32[216,1024]{1,0:T(8,128)}, f32[216,1024]{1,0:T(8,128)}) conditional(s32[]{:T(128)} %clamp.3, (f32[216,1024]{1,0:T(8,128)S(1)}, f32[216,1024]{1,0:T(8,128)S(1)}) %shift.1, (f32[216,1024]{1,0:T(8,128)S(1)}, f32[216,1024]{1,0:T(8,128)S(1)}) %shift.1, (f32[216,1024]{1,0:T(8,128)S(1)}, ...), branch_computations={%region_0.1_spmd, %region_1.2_spmd, %region_2.3_spmd, %region_3.4_... | conditional | bytes 7077984 | solution.py:696
  59.1 12.6 %collective-permute-start.88 = (f32[216,1024]{1,0:T(8,128)S(1)}, f32[216,1024]{1,0:T(8,128)}, u32[]{:S(2)}, u32[]{:S(2)}) collective-permute-start(f32[216,1024]{1,0:T(8,128)S(1)} %get-tuple-element.348), channel_id=1, source_target_pairs={{22,64},{64,22},{23,66},{66,23},{24,68},{68,24},{25,70},{70,25},{2... | collective-permute-start | bytes 2654216 | tf_op jit(solution)/shard_map/cond/branch_44_fun/ppermute | solution.py:311
  71.6 1.6 collective-permute-start.89
  73.2 0.0 collective-permute-done.88
  73.2 0.0 collective-permute-done.89
  73.2 0.0 copy-done.2
  73.2 0.0 copy-done.3
  73.2 0.0 copy-done.5
  73.2 0.0 copy-start.6
  73.3 0.0 copy-start.4
  73.3 18.7 %forward.1 = (f32[3,8,16,2048]{3,2,1,0:T(8,128)}, f32[144,2048]{1,0:T(8,128)S(1)}, f32[32,8,128]{2,1,0:T(8,128)S(1)}) custom-call(s32[1]{0:T(128)} %copy.144.ox_ref, s32[1]{0:T(128)S(6)} %copy.145.oy_ref, f32[3,8,16,2048]{3,2,1,0:T(8,128)} %get-tuple-element.405.prov, f32[216,1024]{1,0:T(8,128)} %get-tuple-element.407.even, ...), custom_call_target="tpu_custom_call" | custom-call | tf_op jit(solution)/shard_map/forward/pallas_call | solution.py:702
  92.0 0.0 copy-done.6
  92.0 85.1 %chain.1.incoming = f32[32,8,128]{2,1,0:T(8,128)S(1)} custom-call(f32[32,8,128]{2,1,0:T(8,128)S(1)} %get-tuple-element.411.ends, f32[16,2,8,128]{3,2,1,0:T(8,128)S(1)} %copy-done.6), custom_call_target="tpu_custom_call" | custom-call | tf_op jit(solution)/shard_map/chain/pallas_call | solution.py:719
  177.0 0.0 copy-done.4
  177.1 17.2 %backward.1 = (f32[3,8,16,2048]{3,2,1,0:T(8,128)}, f32[8,16,2048]{2,1,0:T(8,128)}) custom-call(f32[3,8,16,2048]{3,2,1,0:T(8,128)} %get-tuple-element.409.coupled, f32[144,2048]{1,0:T(8,128)S(1)} %get-tuple-element.410.spectrum, f32[32,8,128]{2,1,0:T(8,128)S(1)} %chain.1.incoming, s32[16,2048]{1,0:T(8,128)S(1)} %bitcast.14, bf16[288,144]{1,0:T(8,128)(2,1)S(1)} %copy-done.4, ...), custom_call_target="tpu_custom_call" | custom-call | tf_op jit(solution)/shard_map/backward/pallas_call | solution.py:728
Async XLA Ops:
  1.9 1.2 copy-start
  3.2 20.4 %copy-start.1 = (s32[1,16,2048]{2,1,0:T(8,128)S(1)}, s32[1,16,2048]{2,1,0:T(8,128)}, u32[]{:S(2)}) copy-start(s32[1,16,2048]{2,1,0:T(8,128)} %param.79) | copy-start | bytes 393220
  3.2 20.4 %copy-start.7 = (bf16[256,128]{1,0:T(8,128)(2,1)S(1)}, bf16[256,128]{1,0:T(8,128)(2,1)}, u32[]{:S(2)}) copy-start(bf16[256,128]{1,0:T(8,128)(2,1)} %constant.39.clone.pair) | copy-start | bytes 196612
  37.6 35.6 %copy-start.2 = (f32[2,8,2048]{2,1,0:T(8,128)S(1)}, f32[2,8,2048]{2,1,0:T(8,128)}, u32[]{:S(2)}) copy-start(f32[2,8,2048]{2,1,0:T(8,128)} %constant.36.clone.modes) | copy-start | bytes 393220
  37.6 35.6 %copy-start.3 = (bf16[2,256,256]{2,1,0:T(8,128)(2,1)S(1)}, bf16[2,256,256]{2,1,0:T(8,128)(2,1)}, u32[]{:S(2)}) copy-start(bf16[2,256,256]{2,1,0:T(8,128)(2,1)} %constant.38.clone.wide_t) | copy-start | bytes 786436
  37.6 35.6 %copy-start.5 = (bf16[288,144]{1,0:T(8,128)(2,1)S(1)}, bf16[288,144]{1,0:T(8,128)(2,1)}, u32[]{:S(2)}) copy-start(bf16[288,144]{1,0:T(8,128)(2,1)} %constant.34.clone.turn_t) | copy-start | bytes 248836
  59.1 14.2 %collective-permute-start.88 = (f32[216,1024]{1,0:T(8,128)S(1)}, f32[216,1024]{1,0:T(8,128)}, u32[]{:S(2)}, u32[]{:S(2)}) collective-permute-start(f32[216,1024]{1,0:T(8,128)S(1)} %get-tuple-element.348), channel_id=1, source_target_pairs={{22,64},{64,22},{23,66},{66,23},{24,68},{68,24},{25,70},{70,25},{2... | collective-permute-start | bytes 2654216 | tf_op jit(solution)/shard_map/cond/branch_44_fun/ppermute | solution.py:311
  71.6 1.6 collective-permute-start.89
  73.2 18.7 %copy-start.6 = (f32[16,2,8,128]{3,2,1,0:T(8,128)S(1)}, f32[16,2,8,128]{3,2,1,0:T(8,128)}, u32[]{:S(2)}) copy-start(f32[16,2,8,128]{3,2,1,0:T(8,128)} %constant.37.clone.jump) | copy-start | bytes 393220
  73.3 103.8 %copy-start.4 = (bf16[288,144]{1,0:T(8,128)(2,1)S(1)}, bf16[288,144]{1,0:T(8,128)(2,1)}, u32[]{:S(2)}) copy-start(bf16[288,144]{1,0:T(8,128)(2,1)} %constant.35.clone.back_t) | copy-start | bytes 248836

commit v3 on v2

--- a/solution.py
+++ b/solution.py
@@ -14,6 +14,7 @@
 ROWS = 16
 LANES = 128
 EXTRA = 144
+TEAM = 8
 DT = 0.2
 BLEND = 0.5
 f32 = jnp.float32
@@ -21,7 +22,7 @@
 VMEM_SPEC = pl.BlockSpec(memory_space=pltpu.VMEM)
 SMEM_SPEC = pl.BlockSpec(memory_space=pltpu.SMEM)
 ANY_SPEC = pl.BlockSpec(memory_space=pl.ANY)
-PARAMS = dict(vmem_limit_bytes=50 * 1024 * 1024)
+MIB = 1024 * 1024
 
 
 def split_np(table):
@@ -69,8 +70,8 @@
     modes = np.stack([root, scale]).astype(np.float32)
     reach = root**ROWS
     tiles = columns // LANES
-    jump = np.stack([reach, 1 / (1 - reach**group)])
-    jump = jump.reshape(2, LEVELS, tiles, LANES).transpose(2, 0, 1, 3).astype(np.float32)
+    jump = np.stack([reach, reach**TEAM, 1 / (1 - reach**group)])
+    jump = jump.reshape(3, LEVELS, tiles, LANES).transpose(0, 2, 1, 3).astype(np.float32)
     wide = np.zeros((2, 256, 256))
     for y in range(256):
         if y % 2 == 0:
@@ -103,7 +104,7 @@
     )
 
 
-def halo_kernel(vel, visc, west, east, edge, sems):
+def halo_kernel(vel_any, visc_any, west, east, vel, visc, edge, sems):
     me = lax.axis_index("gx")
     nest = lax.axis_index("nest")
     group = lax.axis_size("gx")
@@ -111,6 +112,12 @@
     left = lax.rem(me + group - 1, group)
     greet(nest, left)
     greet(nest, right)
+    loads = [pltpu.make_async_copy(vel_any.at[c], vel.at[c], sems.at[4 + c]) for c in range(3)]
+    loads.append(pltpu.make_async_copy(visc_any, visc, sems.at[7]))
+    for load in loads:
+        load.start()
+    for load in loads:
+        load.wait()
     for c in range(3):
         edge[0, c] = vel[c, :, 0, :]
         edge[1, c] = vel[c, :, ROWS - 1, :]
@@ -299,30 +306,120 @@
         lax.fori_loop(0, 24, fill, 0)
 
 
-def cross(shift, group, even, odd):
-    pairs = ([], [])
-    for g in range(group):
-        block = shift + g
-        pairs[block % 2].append((block // 2, group + g))
-        pairs[block % 2].append((group + g, block // 2))
-    if shift < group:
-        pairs[shift % 2].append((2 * group - 1, (shift + group) // 2))
-    axes = ("nest", "gx")
-    return lax.ppermute(even, axes, pairs[0]), lax.ppermute(odd, axes, pairs[1])
+def cross_kernel(shift, even, odd, even_in, odd_in, sems):
+    group = lax.axis_size("gx")
+    me = lax.axis_index("gx")
+    nest = lax.axis_index("nest")
+    barrier = pltpu.get_barrier_semaphore()
+    sources = (even, odd)
+    targets = (even_in, odd_in)
+    means = pl.ds(0, 192)
+    last = group - 1
+    spill = shift < group
+
+    def greet_nest(other, k):
+        pl.semaphore_signal(
+            barrier, inc=1, device_id={"nest": other, "gx": k}, device_id_type=pl.DeviceIdType.MESH
+        )
+
+    @pl.when(nest == 0)
+    def _():
+        for e in range(2):
+            g = 2 * me + e - shift
+
+            @pl.when((g >= 0) & (g < group))
+            def _():
+                greet_nest(1, g)
+
+            if spill:
+                @pl.when(g == group)
+                def _():
+                    greet_nest(1, last)
+
+        count = jnp.int32(0)
+        for e in range(2):
+            g = 2 * me + e - shift
+            count = count + jnp.where((g >= 0) & (g < group), 1, 0)
+
+        @pl.when(count > 0)
+        def _():
+            pl.semaphore_wait(barrier, count)
+
+        for e in range(2):
+            g = 2 * me + e - shift
+
+            @pl.when((g >= 0) & (g < group))
+            def _():
+                remote(sources[e], targets[e], sems.at[0, e], sems.at[1, e], 1, g).start()
+
+        for e in range(2):
+            g = 2 * me + e - shift
+            take = (g >= 0) & (g < group)
+
+            @pl.when(take)
+            def _():
+                await_bytes(sources[e], sems.at[0, e])
+
+            @pl.when(take | (g == group) if spill else take)
+            def _():
+                await_bytes(targets[e].at[means], sems.at[1, e])
+
+    @pl.when(nest == 1)
+    def _():
+        block = shift + me
+        q = block // 2
+        e_mine = lax.rem(block, 2)
+        greet_nest(0, q)
+        pl.semaphore_wait(barrier, jnp.where(me == last, 2, 1) if spill else 1)
+        if spill:
+            @pl.when(me == last)
+            def _():
+                e = shift % 2
+                k = (shift + group) // 2
+                remote(sources[e].at[means], targets[e].at[means], sems.at[0, e], sems.at[1, e], 0, k).start()
+
+        for e in range(2):
+            @pl.when(e_mine == e)
+            def _():
+                remote(sources[e].at[means], targets[e].at[means], sems.at[0, e], sems.at[1, e], 0, q).start()
+
+        for e in range(2):
+            @pl.when(e_mine == e)
+            def _():
+                await_bytes(sources[e].at[means], sems.at[0, e])
+                await_bytes(targets[e], sems.at[1, e])
+
+        if spill:
+            @pl.when(me == last)
+            def _():
+                await_bytes(sources[shift % 2].at[means], sems.at[0, shift % 2])
+
+
+def cross(shift, params, even, odd):
+    return pl.pallas_call(
+        functools.partial(cross_kernel, shift),
+        out_shape=[jax.ShapeDtypeStruct(even.shape, f32)] * 2,
+        in_specs=[VMEM_SPEC] * 2,
+        out_specs=[VMEM_SPEC] * 2,
+        scratch_shapes=[pltpu.SemaphoreType.DMA((2, 2))],
+        compiler_params=params,
+        name="cross",
+    )(even, odd)
 
 
 def forward_kernel(
     ox_ref, oy_ref, prov, even, odd, heights, wide_t, turn_t, modes, y_any,
-    coupled, spectrum, ends, y_t, mapped, wide, rate, source, turned, sem,
+    coupled, spectrum, ends, y_t, mapped, wide, rate, source, turned, sems,
 ):
     columns = prov.shape[-1]
+    loads = [pltpu.make_async_copy(y_any.at[i], y_t.at[i], sems.at[i]) for i in range(4)]
+    for load in loads:
+        load.start()
     group = lax.axis_size("gx")
     x_total = group * ROWS
     half = columns // 2
     tiles = columns // LANES
     blocks = columns // 256
-    load = pltpu.make_async_copy(y_any, y_t, sem)
-    load.start()
     me = lax.axis_index("gx")
     is_child = lax.axis_index("nest") == 1
     ox = ox_ref[0]
@@ -452,7 +549,8 @@
         return carry
 
     lax.fori_loop(0, blocks, turning, 0)
-    load.wait()
+    for load in loads:
+        load.wait()
     width = min(half, 256)
     for part in range(2):
         one = turned[:, pl.ds(0, half)]
@@ -485,93 +583,68 @@
     lax.fori_loop(0, tiles, scans, 0)
 
 
-def chain_kernel(ends, jump, dst, held, result, sems):
+def chain_kernel(ends, jump, dst, held, sums, result, sems):
     me = lax.axis_index("gx")
     nest = lax.axis_index("nest")
-    group = held.shape[0]
-    count = ends.shape[0]
-    tiles = count // 2
-    mine = lax.rem(me, 2) == 0
-    solver = me // 2
-
-    @pl.when(mine)
-    def _():
-        def hello(i, carry):
-            greet(nest, lax.rem(me + i, group))
-            return carry
-
-        lax.fori_loop(1, group, hello, 0)
-        pl.semaphore_wait(pltpu.get_barrier_semaphore(), group - 1)
-
-    @pl.when(jnp.logical_not(mine))
-    def _():
-        def hello(i, carry):
-            greet(nest, 2 * i)
-            return carry
-
-        lax.fori_loop(0, count, hello, 0)
-        pl.semaphore_wait(pltpu.get_barrier_semaphore(), count)
-
-    def send(t, carry):
-        @pl.when(2 * t != me)
-        def _():
-            remote(ends.at[t], held.at[me], sems.at[0], sems.at[1], nest, 2 * t).start()
-
-        return carry
-
-    lax.fori_loop(0, count, send, 0)
-
-    @pl.when(mine)
-    def _():
-        pltpu.make_async_copy(ends.at[solver], held.at[me], sems.at[1]).start()
-        back = solver >= tiles
-        kind = jnp.where(back, solver - tiles, solver)
-        ratio = jump[kind, 0]
-        await_bytes(held, sems.at[1])
-
-        def place(i):
-            return jnp.where(back, group - 1 - i, i)
-
-        def total(i, value):
-            return value * ratio + held[place(i)]
-
-        start = lax.fori_loop(0, group, total, jnp.zeros((8, LANES), f32)) * jump[kind, 1]
-
-        def walk(i, value):
-            g = place(i)
-            result[g] = value
-
-            @pl.when(g != me)
-            def _():
-                remote(result.at[g], dst.at[solver], sems.at[2], sems.at[3], nest, g).start()
-
-            @pl.when(g == me)
-            def _():
-                pltpu.make_async_copy(result.at[g], dst.at[solver], sems.at[3]).start()
-
-            return held[g] + ratio * value
-
-        lax.fori_loop(0, group, walk, start)
-        await_bytes(result.at[pl.ds(0, group - 1)], sems.at[2])
-        await_bytes(ends.at[pl.ds(0, count - 1)], sems.at[0])
-
-    @pl.when(jnp.logical_not(mine))
-    def _():
-        await_bytes(ends, sems.at[0])
-
-    await_bytes(dst, sems.at[3])
+    size, share = ends.shape[:2]
+    teams = sums.shape[0]
+    tiles = jump.shape[1]
+    team = me // size
+    seat = lax.rem(me, size)
+    near = [team * size + lax.rem(seat + i, size) for i in range(1, size)]
+    far = [lax.rem(team + i, teams) * size + seat for i in range(1, teams)]
+    for k in near + far:
+        greet(nest, k)
+    pl.semaphore_wait(pltpu.get_barrier_semaphore(), len(near) + len(far))
+    for i in range(1, size):
+        other = lax.rem(seat + i, size)
+        remote(ends.at[other], held.at[seat], sems.at[0], sems.at[1], nest, team * size + other).start()
+    held[seat] = ends[seat]
+    first = seat * share
+    back = first >= tiles
+    own = pl.ds(jnp.where(back, first - tiles, first), share)
+    ratio = jump[0, own]
+    await_bytes(held.at[pl.ds(0, size - 1)], sems.at[1])
+
+    def place(i):
+        return jnp.where(back, size - 1 - i, i)
+
+    total = held[place(0)]
+    for i in range(1, size):
+        total = total * ratio + held[place(i)]
+    sums[team] = total
+    for i in range(1, teams):
+        k = lax.rem(team + i, teams) * size + seat
+        remote(sums.at[team], sums.at[team], sems.at[2], sems.at[3], nest, k).start()
+    await_bytes(sums.at[pl.ds(0, teams - 1)], sems.at[3])
+    value = total
+    for i in range(1, teams):
+        at = jnp.where(back, lax.rem(team + teams - i, teams), lax.rem(team + i, teams))
+        value = value * jump[1, own] + sums[at]
+    value = value * jump[2, own]
+    for i in range(size):
+        g = place(i)
+        result[g] = value
+        if i < size - 1:
+            value = held[g] + ratio * value
+    for i in range(1, size):
+        other = lax.rem(seat + i, size)
+        remote(result.at[other], dst.at[seat], sems.at[4], sems.at[5], nest, team * size + other).start()
+    dst[seat] = result[seat]
+    await_bytes(ends.at[pl.ds(0, size - 1)], sems.at[0])
+    await_bytes(sums.at[pl.ds(0, teams - 1)], sems.at[2])
+    await_bytes(result.at[pl.ds(0, size - 1)], sems.at[4])
+    await_bytes(dst.at[pl.ds(0, size - 1)], sems.at[5])
 
 
 def backward_kernel(
-    coupled, spectrum, incoming, heights, back_t, modes, y_any,
-    updated, pressure, y_t, waves, folded, east, sem,
+    coupled, spectrum, incoming, heights, back_t, modes, y_t,
+    updated, pressure, waves, folded, east,
 ):
     columns = coupled.shape[-1]
     half = columns // 2
     tiles = columns // LANES
     blocks = columns // 256
-    load = pltpu.make_async_copy(y_any, y_t, sem)
-    load.start()
     waves[pl.ds(8 * (ROWS + 1), 8), :] = jnp.zeros((8, columns), f32)
 
     def scans(t, carry):
@@ -592,7 +665,6 @@
         return carry
 
     lax.fori_loop(0, tiles, scans, 0)
-    load.wait()
     width = min(half, 256)
     parts = []
     for part in range(2):
@@ -652,19 +724,21 @@
     tiles = columns // LANES
     half = columns // 2
     t = {name: jnp.asarray(value) for name, value in tables(x_total, columns, group).items()}
-    params = pltpu.CompilerParams(**PARAMS)
-    effects = lambda number: pltpu.CompilerParams(has_side_effects=True, collective_id=number, **PARAMS)
+    params = lambda size: pltpu.CompilerParams(vmem_limit_bytes=size * MIB)
+    effects = lambda number, size: pltpu.CompilerParams(
+        has_side_effects=True, collective_id=number, vmem_limit_bytes=size * MIB
+    )
     shape = lambda *dims: jax.ShapeDtypeStruct(dims, f32)
     vmem = pltpu.VMEM
     dma = pltpu.SemaphoreType.DMA
 
-    west, east = pl.pallas_call(
+    west, east, flow, viscous = pl.pallas_call(
         halo_kernel,
-        out_shape=[shape(4, LEVELS, columns)] * 2,
-        in_specs=[VMEM_SPEC] * 2,
-        out_specs=[VMEM_SPEC] * 2,
-        scratch_shapes=[vmem((2, 4, LEVELS, columns), f32), dma((4,))],
-        compiler_params=effects(0),
+        out_shape=[shape(4, LEVELS, columns)] * 2 + [shape(*flow.shape), shape(*viscous.shape)],
+        in_specs=[ANY_SPEC] * 2,
+        out_specs=[VMEM_SPEC] * 4,
+        scratch_shapes=[vmem((2, 4, LEVELS, columns), f32), dma((8,))],
+        compiler_params=effects(0, 10),
         name="halo",
     )(flow, viscous)
     prov, chunks = pl.pallas_call(
@@ -673,7 +747,7 @@
         in_specs=[SMEM_SPEC] + [VMEM_SPEC] * 6,
         out_specs=[VMEM_SPEC] * 2,
         scratch_shapes=[vmem((24 * 8, columns), f32), vmem((tiles, ROWS, LANES), f32)],
-        compiler_params=params,
+        compiler_params=params(14),
         name="stencil",
     )(column_offset, flow, viscous, roofs, west, east, t["pair"])
     beside = pl.pallas_call(
@@ -682,7 +756,7 @@
         in_specs=[VMEM_SPEC],
         out_specs=VMEM_SPEC,
         scratch_shapes=[dma((2,))],
-        compiler_params=effects(1),
+        compiler_params=effects(1, 6),
         name="align",
     )(chunks)
     even, odd = pl.pallas_call(
@@ -690,56 +764,65 @@
         out_shape=[shape(216, half)] * 2,
         in_specs=[SMEM_SPEC] + [VMEM_SPEC] * 2,
         out_specs=[VMEM_SPEC] * 2,
-        compiler_params=params,
+        compiler_params=params(8),
         name="shift",
     )(row_offset, chunks, beside)
     even, odd = lax.switch(
         row_offset[0] // 8,
-        [functools.partial(cross, number, group) for number in range(group + 1)],
+        [functools.partial(cross, number, effects(3 + number, 6)) for number in range(group + 1)],
         even,
         odd,
     )
-    coupled, spectrum, ends = pl.pallas_call(
+    coupled, spectrum, ends, y_t = pl.pallas_call(
         forward_kernel,
-        out_shape=[shape(3, LEVELS, ROWS, columns), shape(EXTRA, columns), shape(2 * tiles, 8, LANES)],
+        out_shape=[
+            shape(3, LEVELS, ROWS, columns),
+            shape(EXTRA, columns),
+            shape(2 * tiles, 8, LANES),
+            jax.ShapeDtypeStruct((4, half, half), bf16),
+        ],
         in_specs=[SMEM_SPEC] * 2 + [VMEM_SPEC] * 7 + [ANY_SPEC],
-        out_specs=[VMEM_SPEC] * 3,
+        out_specs=[VMEM_SPEC] * 4,
         scratch_shapes=[
-            vmem((4, half, half), bf16),
             vmem((24, tiles, ROWS, LANES), f32),
             vmem((216, columns), f32),
             vmem((ROWS, columns), f32),
             vmem((EXTRA, columns), f32),
             vmem((EXTRA, columns), f32),
-            dma(()),
+            dma((4,)),
         ],
-        compiler_params=params,
+        compiler_params=params(32),
         name="forward",
     )(row_offset, column_offset, prov, even, odd, roofs, t["wide"], t["turn"], t["modes"], t["y"])
+    share = 2 * tiles // TEAM
     incoming = pl.pallas_call(
         chain_kernel,
-        out_shape=shape(2 * tiles, 8, LANES),
+        out_shape=shape(TEAM, share, 8, LANES),
         in_specs=[VMEM_SPEC] * 2,
         out_specs=VMEM_SPEC,
-        scratch_shapes=[vmem((group, 8, LANES), f32), vmem((group, 8, LANES), f32), dma((4,))],
-        compiler_params=effects(2),
+        scratch_shapes=[
+            vmem((TEAM, share, 8, LANES), f32),
+            vmem((group // TEAM, share, 8, LANES), f32),
+            vmem((TEAM, share, 8, LANES), f32),
+            dma((6,)),
+        ],
+        compiler_params=effects(2, 4),
         name="chain",
-    )(ends, t["jump"])
+    )(ends.reshape(TEAM, share, 8, LANES), t["jump"])
+    incoming = incoming.reshape(2 * tiles, 8, LANES)
     updated, pressure = pl.pallas_call(
         backward_kernel,
         out_shape=[shape(3, LEVELS, ROWS, columns), shape(LEVELS, ROWS, columns)],
-        in_specs=[VMEM_SPEC] * 6 + [ANY_SPEC],
+        in_specs=[VMEM_SPEC] * 7,
         out_specs=[VMEM_SPEC] * 2,
         scratch_shapes=[
-            vmem((4, half, half), bf16),
             vmem((EXTRA, columns), f32),
             vmem((EXTRA, columns), f32),
             vmem((LEVELS, columns), f32),
-            dma(()),
         ],
-        compiler_params=params,
+        compiler_params=params(24),
         name="backward",
-    )(coupled, spectrum, incoming, roofs, t["back"], t["modes"], t["y"])
+    )(coupled, spectrum, incoming, roofs, t["back"], t["modes"], y_t)
     return updated[None], pressure[None]
 
 

time: 195 us -> 151 us (0.77)
  Pallas kernels: 177 us -> 145 us
  starting transfers between devices: 14.2 us -> 0 us
  local copies, waits for them, and re-layouts: 1.25 us -> 4.08 us
    ppermute x2 -> x0, starting transfers between devices: 14.2 us -> none  [the longest x1 12.6 us: cross(): lax.ppermute(even, axes, pairs[0])]
    pallas_call x2 -> x3, Pallas kernels: 105 us -> 93.5 us  [the longest x1 82.8 us: local(): pl.pallas_call(chain_kernel, out_shape=shape(TEAM, share, 8, LANES), in_s...]
    pallas_call x1, Pallas kernels: 20.9 us -> 11.5 us  [local(): pl.pallas_call(align_kernel, out_shape=shape(24, 8, half), in_specs=[VMEM...]
    pallas_call x1, Pallas kernels: 17.2 us -> 12.5 us  [local(): pl.pallas_call(backward_kernel, out_shape=[shape(3, LEVELS, ROWS, columns...]
    pallas_call x1, Pallas kernels: 14 us -> 10.5 us  [local(): pl.pallas_call(stencil_kernel, out_shape=[shape(3, LEVELS, ROWS, columns)...]
    unnamed x16 -> x18, local copies, waits for them, and re-layouts: 1.25 us -> 4.08 us
    pallas_call x1, Pallas kernels: 18.7 us -> 16.1 us  [local(): pl.pallas_call(forward_kernel, out_shape=[shape(3, LEVELS, ROWS, columns)...]
  transfers between devices with their start and end apart: 2 -> 0, of which waited for: 0 -> 0; matrix products, arithmetic and copies ran while one was open for 0% -> 0% of each run, Pallas kernels for 0% -> 0%
where the time goes in v3:
time: 151 us
  Pallas kernels  145 us (96%)
  local copies, waits for them, and re-layouts  4.08 us (3%)
  between operations  2.09 us (1%)
    pallas_call x1, Pallas kernels, local(): pl.pallas_call(chain_kernel, out_shape=shape(TEAM, share, 8, LANES), in_s...  82.8 us
    pallas_call x1, Pallas kernels, local(): pl.pallas_call(forward_kernel, out_shape=[shape(3, LEVELS, ROWS, columns)...  16.1 us
    pallas_call x1, Pallas kernels, local(): pl.pallas_call(backward_kernel, out_shape=[shape(3, LEVELS, ROWS, columns...  12.5 us
    pallas_call x1, Pallas kernels, local(): pl.pallas_call(align_kernel, out_shape=shape(24, 8, half), in_specs=[VMEM...  11.5 us
    pallas_call x1, Pallas kernels, local(): pl.pallas_call(stencil_kernel, out_shape=[shape(3, LEVELS, ROWS, columns)...  10.5 us
    pallas_call x1, Pallas kernels, local(): pl.pallas_call(halo_kernel, out_shape=[shape(4, LEVELS, columns)] * 2 + [...  9.29 us
    unnamed x18, local copies, waits for them, and re-layouts  4.08 us

profile of v3, /device:TPU:1, one launch (start us, length us, event | category | flops | bytes accessed | tf_op | source)
XLA Modules:
  0.0 151.1 jit_solution(3696273178156413866)
XLA Ops:
  1.9 0.0 copy-start
  2.0 1.9 %copy-done = f32[1,3,8,16,2048]{4,3,2,1,0:T(8,128)S(1)} copy-done((f32[1,3,8,16,2048]{4,3,2,1,0:T(8,128)S(1)}, f32[1,3,8,16,2048]{4,3,2,1,0:T(8,128)}, u32[]{:S(2)}) %copy-start) | copy-done | bytes 3145752
  3.8 0.0 copy-start.2
  3.8 1.2 copy-done.2
  5.1 0.0 copy-start.1
  5.1 0.0 copy-start.8
  5.1 9.3 %halo.1 = (f32[4,8,2048]{2,1,0:T(8,128)S(1)}, f32[4,8,2048]{2,1,0:T(8,128)S(1)}, f32[3,8,16,2048]{3,2,1,0:T(8,128)S(1)}, f32[8,16,2048]{2,1,0:T(8,128)S(1)}) custom-call(f32[3,8,16,2048]{3,2,1,0:T(8,128)S(1)} %bitcast.12, f32[8,16,2048]{2,1,0:T(8,128)S(1)} %bitcast.16), custom_call_target="tpu_custom_call" | custom-call | tf_op jit(solution)/shard_map/halo/pallas_call | solution.py:735
  14.4 0.0 copy-done.1
  14.4 0.0 copy-done.8
  14.4 10.5 %stencil.1 = (f32[3,8,16,2048]{3,2,1,0:T(8,128)S(1)}, f32[24,16,1024]{2,1,0:T(8,128)S(1)}) custom-call(s32[1]{0:T(128)S(6)} %copy.145.oy_ref, f32[3,8,16,2048]{3,2,1,0:T(8,128)S(1)} %get-tuple-element.406.vel, f32[8,16,2048]{2,1,0:T(8,128)S(1)} %get-tuple-element.407.visc, s32[16,2048]{1,0:T(8,128)S(1)} %bitcast.13, ...), custom_call_target="tpu_custom_call" | custom-call | tf_op jit(solution)/shard_map/stencil/pallas_call | solution.py:744
  24.9 11.5 %align.1.beside = f32[24,8,1024]{2,1,0:T(8,128)S(1)} custom-call(f32[24,16,1024]{2,1,0:T(8,128)S(1)} %get-tuple-element.411.src.own), custom_call_target="tpu_custom_call" | custom-call | tf_op jit(solution)/shard_map/align/pallas_call | solution.py:753
  36.4 0.5 shift.1
  36.9 0.0 copy-start.3
  36.9 0.0 copy-start.7
  36.9 1.7 %conditional.1 = ((f32[216,1024]{1,0:T(8,128)}, f32[216,1024]{1,0:T(8,128)})) conditional(s32[]{:T(128)} %clamp.3, (f32[216,1024]{1,0:T(8,128)S(1)}, f32[216,1024]{1,0:T(8,128)S(1)}) %shift.1, (f32[216,1024]{1,0:T(8,128)S(1)}, f32[216,1024]{1,0:T(8,128)S(1)}) %shift.1, (f32[216,1024]{1,0:T(8,128)S(1)}, ...), branch_computations={%region_0.1_spmd, %region_1.2_spmd, %region_2.3_spmd, %region_3.4_... | conditional | bytes 8 | solution.py:770
  37.0 1.4 cross.89
  38.6 0.0 copy-done.3
  38.6 0.0 copy-done.7
  38.6 0.0 copy-start.4
  38.7 0.9 copy-done.4
  39.6 0.0 copy-start.5
  39.6 0.0 copy-start.6
  39.6 16.1 %forward.1 = (f32[3,8,16,2048]{3,2,1,0:T(8,128)S(1)}, f32[144,2048]{1,0:T(8,128)S(1)}, f32[32,8,128]{2,1,0:T(8,128)S(1)}, bf16[4,1024,1024]{2,1,0:T(8,128)(2,1)S(1)}) custom-call(s32[1]{0:T(128)} %copy.144.ox_ref, s32[1]{0:T(128)S(6)} %copy.145.oy_ref, f32[3,8,16,2048]{3,2,1,0:T(8,128)S(1)} %get-tuple-element.410.prov, f32[216,1024]{1,0:T(8,128)} %get-tuple-element.412.even, ...), custom_call_target="tpu_custom_call" | custom-call | tf_op jit(solution)/shard_map/forward/pallas_call | solution.py:776
  55.7 0.0 copy-done.5
  55.7 82.8 %chain.1 = f32[8,4,8,128]{3,2,1,0:T(8,128)S(1)} custom-call(f32[8,4,8,128]{3,2,1,0:T(8,128)S(1)} %bitcast.18, f32[3,16,8,128]{3,2,1,0:T(8,128)S(1)} %copy-done.5), custom_call_target="tpu_custom_call" | custom-call | tf_op jit(solution)/shard_map/chain/pallas_call | solution.py:798
  138.5 0.0 copy-done.6
  138.5 12.5 %backward.1 = (f32[3,8,16,2048]{3,2,1,0:T(8,128)}, f32[8,16,2048]{2,1,0:T(8,128)}) custom-call(f32[3,8,16,2048]{3,2,1,0:T(8,128)S(1)} %get-tuple-element.414.coupled, f32[144,2048]{1,0:T(8,128)S(1)} %get-tuple-element.415.spectrum, f32[32,8,128]{2,1,0:T(8,128)S(1)} %bitcast.17, s32[16,2048]{1,0:T(8,128)S(1)} %bitcast.15, bf16[288,144]{1,0:T(8,128)(2,1)S(1)} %copy-done.6, ...), custom_call_target="tpu_custom_call" | custom-call | tf_op jit(solution)/shard_map/backward/pallas_call | solution.py:813
Async XLA Ops:
  1.9 1.9 %copy-start = (f32[1,3,8,16,2048]{4,3,2,1,0:T(8,128)S(1)}, f32[1,3,8,16,2048]{4,3,2,1,0:T(8,128)}, u32[]{:S(2)}) copy-start(f32[1,3,8,16,2048]{4,3,2,1,0:T(8,128)} %param.77) | copy-start | bytes 9437188
  3.8 1.2 copy-start.2
  5.1 9.3 %copy-start.1 = (s32[1,16,2048]{2,1,0:T(8,128)S(1)}, s32[1,16,2048]{2,1,0:T(8,128)}, u32[]{:S(2)}) copy-start(s32[1,16,2048]{2,1,0:T(8,128)} %param.79) | copy-start | bytes 393220
  5.1 9.3 %copy-start.8 = (bf16[256,128]{1,0:T(8,128)(2,1)S(1)}, bf16[256,128]{1,0:T(8,128)(2,1)}, u32[]{:S(2)}) copy-start(bf16[256,128]{1,0:T(8,128)(2,1)} %constant.39.clone.pair) | copy-start | bytes 196612
  36.9 1.7 %copy-start.3 = (f32[2,8,2048]{2,1,0:T(8,128)S(1)}, f32[2,8,2048]{2,1,0:T(8,128)}, u32[]{:S(2)}) copy-start(f32[2,8,2048]{2,1,0:T(8,128)} %constant.36.clone.modes) | copy-start | bytes 393220
  36.9 1.7 %copy-start.7 = (bf16[288,144]{1,0:T(8,128)(2,1)S(1)}, bf16[288,144]{1,0:T(8,128)(2,1)}, u32[]{:S(2)}) copy-start(bf16[288,144]{1,0:T(8,128)(2,1)} %constant.34.clone.turn_t) | copy-start | bytes 248836
  38.6 1.0 copy-start.4
  39.6 16.1 %copy-start.5 = (f32[3,16,8,128]{3,2,1,0:T(8,128)S(1)}, f32[3,16,8,128]{3,2,1,0:T(8,128)}, u32[]{:S(2)}) copy-start(f32[3,16,8,128]{3,2,1,0:T(8,128)} %constant.37.clone.jump) | copy-start | bytes 589828
  39.6 98.9 %copy-start.6 = (bf16[288,144]{1,0:T(8,128)(2,1)S(1)}, bf16[288,144]{1,0:T(8,128)(2,1)}, u32[]{:S(2)}) copy-start(bf16[288,144]{1,0:T(8,128)(2,1)} %constant.35.clone.back_t) | copy-start | bytes 248836

commit v4 on v3

--- a/solution.py
+++ b/solution.py
@@ -192,7 +192,7 @@
             prov[c, z, :, here] = value * mask
         return carry
 
-    lax.fori_loop(0, LEVELS * blocks, cell, 0)
+    lax.fori_loop(0, LEVELS * blocks, cell, 0, unroll=2)
 
     @pl.when(jnp.logical_not(is_child))
     def _():
@@ -212,7 +212,7 @@
                 out[cz, :, pl.ds(b * LANES, LANES)] = jnp.where(lane < LANES - shift, moved[b], moved[b + 1])
             return carry
 
-        lax.fori_loop(0, 24, unit, 0)
+        lax.fori_loop(0, 24, unit, 0, unroll=2)
 
     @pl.when(is_child)
     def _():
@@ -490,7 +490,7 @@
                 mapped[cz, lax.rem(first + b, tiles)] = jnp.where(lane >= shift, own, before)
             return carry
 
-        lax.fori_loop(0, 24, unit, 0)
+        lax.fori_loop(0, 24, unit, 0, unroll=2)
 
         def rates(t, carry):
             cols = pl.ds(pl.multiple_of(t * LANES, LANES), LANES)
@@ -519,7 +519,7 @@
             coupled[c, z, :, cols] = (own + weight * change) * mask
         return carry
 
-    lax.fori_loop(0, LEVELS * blocks, blend, 0)
+    lax.fori_loop(0, LEVELS * blocks, blend, 0, unroll=4)
     row2 = lax.broadcasted_iota(jnp.int32, (ROWS, 256), 0)
 
     def diverge(i, carry):
@@ -539,7 +539,7 @@
         source[pl.ds(ROWS * LEVELS + z, 1), cols] = flow_x[ROWS - 1 :] * (-1.0 / DT)
         return carry
 
-    lax.fori_loop(0, LEVELS * blocks, diverge, 0)
+    lax.fori_loop(0, LEVELS * blocks, diverge, 0, unroll=4)
 
     def turning(b, carry):
         cols = pl.ds(pl.multiple_of(b * 256, 256), 256)
@@ -639,7 +639,7 @@
 
 def backward_kernel(
     coupled, spectrum, incoming, heights, back_t, modes, y_t,
-    updated, pressure, waves, folded, east,
+    updated_out, pressure_out, waves, folded, east, updated, pressure, sems,
 ):
     columns = coupled.shape[-1]
     half = columns // 2
@@ -694,26 +694,31 @@
         return carry
 
     lax.fori_loop(0, blocks, turning, 0)
+    stores = [pltpu.make_async_copy(pressure, pressure_out, sems.at[LEVELS])]
+    stores[0].start()
     row = lax.broadcasted_iota(jnp.int32, (ROWS, 256), 0)
 
-    def project(i, carry):
-        z = i // blocks
-        start = pl.multiple_of(lax.rem(i, blocks) * 256, 256)
+    def project(z, b, carry):
+        start = pl.multiple_of(b * 256, 256)
         cols = pl.ds(start, 256)
         after = pl.ds(pl.multiple_of(lax.rem(start + 256, columns), LANES), LANES)
         own = pressure[z, :, cols]
         beyond = jnp.concatenate([own, pressure[z, :, after]], axis=1)
         north = pltpu.roll(beyond, 383, 1)[:, :256]
         plus = jnp.where(row == ROWS - 1, east[pl.ds(z, 1), cols], pltpu.roll(own, ROWS - 1, 0))
-        top = pressure[jnp.minimum(z + 1, LEVELS - 1), :, cols]
-        top = top * jnp.where(z < LEVELS - 1, 1.0, 0.0).astype(f32)
+        top = pressure[z + 1, :, cols] if z < LEVELS - 1 else jnp.zeros_like(own)
         mask = jnp.where(z >= heights[:, cols], 1.0, 0.0).astype(f32)
         updated[0, z, :, cols] = mask * (coupled[0, z, :, cols] - DT * (plus - own))
         updated[1, z, :, cols] = mask * (coupled[1, z, :, cols] - DT * (north - own))
         updated[2, z, :, cols] = mask * (coupled[2, z, :, cols] - DT * (top - own))
         return carry
 
-    lax.fori_loop(0, LEVELS * blocks, project, 0)
+    for z in range(LEVELS):
+        lax.fori_loop(0, blocks, functools.partial(project, z), 0, unroll=2)
+        stores.append(pltpu.make_async_copy(updated.at[:, z], updated_out.at[:, z], sems.at[z]))
+        stores[-1].start()
+    for store in stores:
+        store.wait()
 
 
 def local(velocity, viscosity, heights, row_offset, column_offset):
@@ -814,11 +819,14 @@
         backward_kernel,
         out_shape=[shape(3, LEVELS, ROWS, columns), shape(LEVELS, ROWS, columns)],
         in_specs=[VMEM_SPEC] * 7,
-        out_specs=[VMEM_SPEC] * 2,
+        out_specs=[ANY_SPEC] * 2,
         scratch_shapes=[
             vmem((EXTRA, columns), f32),
             vmem((EXTRA, columns), f32),
             vmem((LEVELS, columns), f32),
+            vmem((3, LEVELS, ROWS, columns), f32),
+            vmem((LEVELS, ROWS, columns), f32),
+            dma((LEVELS + 1,)),
         ],
         compiler_params=params(24),
         name="backward",

time: 151 us -> 133 us (0.88); the launches traced: 151 us -> 135 us
  Pallas kernels: 145 us -> 129 us
    pallas_call x1, Pallas kernels: 82.8 us -> 65.2 us  [local(): pl.pallas_call(chain_kernel, out_shape=shape(TEAM, share, 8, LANES), in_s...]
    pallas_call x1, Pallas kernels: 1.41 us -> 14.6 us  [cross(): pl.pallas_call(functools.partial(cross_kernel, shift), out_shape=[jax.Sha...]
    pallas_call x1, Pallas kernels: 16.1 us -> 11.5 us  [local(): pl.pallas_call(forward_kernel, out_shape=[shape(3, LEVELS, ROWS, columns)...]
    pallas_call x1, Pallas kernels: 12.5 us -> 8.77 us  [local(): pl.pallas_call(backward_kernel, out_shape=[shape(3, LEVELS, ROWS, columns...]
    pallas_call x1, Pallas kernels: 10.5 us -> 7.5 us  [local(): pl.pallas_call(stencil_kernel, out_shape=[shape(3, LEVELS, ROWS, columns)...]
where the time goes in v4:
time: 133 us; the launch traced here: 135 us
  Pallas kernels  129 us (97%)
  local copies, waits for them, and re-layouts  4.08 us (3%)
  between operations  2.25 us (2%)
    pallas_call x1, Pallas kernels, local(): pl.pallas_call(chain_kernel, out_shape=shape(TEAM, share, 8, LANES), in_s...  65.2 us
    pallas_call x1, Pallas kernels, cross(): pl.pallas_call(functools.partial(cross_kernel, shift), out_shape=[jax.Sha...  14.6 us
    pallas_call x1, Pallas kernels, local(): pl.pallas_call(align_kernel, out_shape=shape(24, 8, half), in_specs=[VMEM...  11.5 us
    pallas_call x1, Pallas kernels, local(): pl.pallas_call(forward_kernel, out_shape=[shape(3, LEVELS, ROWS, columns)...  11.5 us
    pallas_call x1, Pallas kernels, local(): pl.pallas_call(halo_kernel, out_shape=[shape(4, LEVELS, columns)] * 2 + [...  9.29 us
    pallas_call x1, Pallas kernels, local(): pl.pallas_call(backward_kernel, out_shape=[shape(3, LEVELS, ROWS, columns...  8.77 us
    pallas_call x1, Pallas kernels, local(): pl.pallas_call(stencil_kernel, out_shape=[shape(3, LEVELS, ROWS, columns)...  7.5 us
    unnamed x18, local copies, waits for them, and re-layouts  4.08 us

profile of v4, /device:TPU:1, one launch (start us, length us, event | category | flops | bytes accessed | tf_op | source)
XLA Modules:
  0.0 135.4 jit_solution(17434902110653029835)
XLA Ops:
  1.9 0.0 copy-start
  2.0 1.9 %copy-done = f32[1,3,8,16,2048]{4,3,2,1,0:T(8,128)S(1)} copy-done((f32[1,3,8,16,2048]{4,3,2,1,0:T(8,128)S(1)}, f32[1,3,8,16,2048]{4,3,2,1,0:T(8,128)}, u32[]{:S(2)}) %copy-start) | copy-done | bytes 3145752
  3.8 0.0 copy-start.2
  3.8 1.2 copy-done.2
  5.1 0.0 copy-start.1
  5.1 0.0 copy-start.8
  5.1 9.3 %halo.1 = (f32[4,8,2048]{2,1,0:T(8,128)S(1)}, f32[4,8,2048]{2,1,0:T(8,128)S(1)}, f32[3,8,16,2048]{3,2,1,0:T(8,128)S(1)}, f32[8,16,2048]{2,1,0:T(8,128)S(1)}) custom-call(f32[3,8,16,2048]{3,2,1,0:T(8,128)S(1)} %bitcast.12, f32[8,16,2048]{2,1,0:T(8,128)S(1)} %bitcast.16), custom_call_target="tpu_custom_call" | custom-call | tf_op jit(solution)/shard_map/halo/pallas_call | solution.py:740
  14.4 0.0 copy-done.1
  14.4 0.0 copy-done.8
  14.4 7.5 %stencil.1 = (f32[3,8,16,2048]{3,2,1,0:T(8,128)S(1)}, f32[24,16,1024]{2,1,0:T(8,128)S(1)}) custom-call(s32[1]{0:T(128)S(6)} %copy.145.oy_ref, f32[3,8,16,2048]{3,2,1,0:T(8,128)S(1)} %get-tuple-element.406.vel, f32[8,16,2048]{2,1,0:T(8,128)S(1)} %get-tuple-element.407.visc, s32[16,2048]{1,0:T(8,128)S(1)} %bitcast.13, ...), custom_call_target="tpu_custom_call" | custom-call | tf_op jit(solution)/shard_map/stencil/pallas_call | solution.py:749
  21.9 11.5 %align.1.beside = f32[24,8,1024]{2,1,0:T(8,128)S(1)} custom-call(f32[24,16,1024]{2,1,0:T(8,128)S(1)} %get-tuple-element.411.src.own), custom_call_target="tpu_custom_call" | custom-call | tf_op jit(solution)/shard_map/align/pallas_call | solution.py:758
  33.4 0.5 shift.1
  33.9 0.0 copy-start.3
  33.9 0.0 copy-start.7
  34.0 14.8 %conditional.1 = ((f32[216,1024]{1,0:T(8,128)}, f32[216,1024]{1,0:T(8,128)})) conditional(s32[]{:T(128)} %clamp.3, (f32[216,1024]{1,0:T(8,128)S(1)}, f32[216,1024]{1,0:T(8,128)S(1)}) %shift.1, (f32[216,1024]{1,0:T(8,128)S(1)}, f32[216,1024]{1,0:T(8,128)S(1)}) %shift.1, (f32[216,1024]{1,0:T(8,128)S(1)}, ...), branch_computations={%region_0.1_spmd, %region_1.2_spmd, %region_2.3_spmd, %region_3.4_... | conditional | bytes 8 | solution.py:775
  34.0 14.6 %cross.98 = (f32[216,1024]{1,0:T(8,128)}, f32[216,1024]{1,0:T(8,128)}) custom-call(f32[216,1024]{1,0:T(8,128)S(1)} %get-tuple-element.326.even, f32[216,1024]{1,0:T(8,128)S(1)} %get-tuple-element.327.odd), custom_call_target="tpu_custom_call" | custom-call | tf_op jit(solution)/shard_map/cond/branch_33_fun/cross/pallas_call | solution.py:399
  48.8 0.0 copy-done.3
  48.8 0.0 copy-done.7
  48.8 0.0 copy-start.4
  48.8 0.9 copy-done.4
  49.8 0.0 copy-start.5
  49.8 0.0 copy-start.6
  49.8 11.5 %forward.1 = (f32[3,8,16,2048]{3,2,1,0:T(8,128)S(1)}, f32[144,2048]{1,0:T(8,128)S(1)}, f32[32,8,128]{2,1,0:T(8,128)S(1)}, bf16[4,1024,1024]{2,1,0:T(8,128)(2,1)S(1)}) custom-call(s32[1]{0:T(128)} %copy.144.ox_ref, s32[1]{0:T(128)S(6)} %copy.145.oy_ref, f32[3,8,16,2048]{3,2,1,0:T(8,128)S(1)} %get-tuple-element.410.prov, f32[216,1024]{1,0:T(8,128)} %get-tuple-element.412.even, ...), custom_call_target="tpu_custom_call" | custom-call | tf_op jit(solution)/shard_map/forward/pallas_call | solution.py:781
  61.2 0.0 copy-done.5
  61.2 65.2 %chain.1 = f32[8,4,8,128]{3,2,1,0:T(8,128)S(1)} custom-call(f32[8,4,8,128]{3,2,1,0:T(8,128)S(1)} %bitcast.18, f32[3,16,8,128]{3,2,1,0:T(8,128)S(1)} %copy-done.5), custom_call_target="tpu_custom_call" | custom-call | tf_op jit(solution)/shard_map/chain/pallas_call | solution.py:803
  126.5 0.0 copy-done.6
  126.5 8.8 %backward.1 = (f32[3,8,16,2048]{3,2,1,0:T(8,128)}, f32[8,16,2048]{2,1,0:T(8,128)}) custom-call(f32[3,8,16,2048]{3,2,1,0:T(8,128)S(1)} %get-tuple-element.414.coupled, f32[144,2048]{1,0:T(8,128)S(1)} %get-tuple-element.415.spectrum, f32[32,8,128]{2,1,0:T(8,128)S(1)} %bitcast.17, s32[16,2048]{1,0:T(8,128)S(1)} %bitcast.15, bf16[288,144]{1,0:T(8,128)(2,1)S(1)} %copy-done.6, ...), custom_call_target="tpu_custom_call" | custom-call | tf_op jit(solution)/shard_map/backward/pallas_call | solution.py:818
Async XLA Ops:
  1.9 1.9 %copy-start = (f32[1,3,8,16,2048]{4,3,2,1,0:T(8,128)S(1)}, f32[1,3,8,16,2048]{4,3,2,1,0:T(8,128)}, u32[]{:S(2)}) copy-start(f32[1,3,8,16,2048]{4,3,2,1,0:T(8,128)} %param.77) | copy-start | bytes 9437188
  3.8 1.2 copy-start.2
  5.1 9.3 %copy-start.1 = (s32[1,16,2048]{2,1,0:T(8,128)S(1)}, s32[1,16,2048]{2,1,0:T(8,128)}, u32[]{:S(2)}) copy-start(s32[1,16,2048]{2,1,0:T(8,128)} %param.79) | copy-start | bytes 393220
  5.1 9.3 %copy-start.8 = (bf16[256,128]{1,0:T(8,128)(2,1)S(1)}, bf16[256,128]{1,0:T(8,128)(2,1)}, u32[]{:S(2)}) copy-start(bf16[256,128]{1,0:T(8,128)(2,1)} %constant.39.clone.pair) | copy-start | bytes 196612
  33.9 14.9 %copy-start.3 = (f32[2,8,2048]{2,1,0:T(8,128)S(1)}, f32[2,8,2048]{2,1,0:T(8,128)}, u32[]{:S(2)}) copy-start(f32[2,8,2048]{2,1,0:T(8,128)} %constant.36.clone.modes) | copy-start | bytes 393220
  33.9 14.9 %copy-start.7 = (bf16[288,144]{1,0:T(8,128)(2,1)S(1)}, bf16[288,144]{1,0:T(8,128)(2,1)}, u32[]{:S(2)}) copy-start(bf16[288,144]{1,0:T(8,128)(2,1)} %constant.34.clone.turn_t) | copy-start | bytes 248836
  48.8 1.0 copy-start.4
  49.8 11.5 %copy-start.5 = (f32[3,16,8,128]{3,2,1,0:T(8,128)S(1)}, f32[3,16,8,128]{3,2,1,0:T(8,128)}, u32[]{:S(2)}) copy-start(f32[3,16,8,128]{3,2,1,0:T(8,128)} %constant.37.clone.jump) | copy-start | bytes 589828
  49.8 76.7 %copy-start.6 = (bf16[288,144]{1,0:T(8,128)(2,1)S(1)}, bf16[288,144]{1,0:T(8,128)(2,1)}, u32[]{:S(2)}) copy-start(bf16[288,144]{1,0:T(8,128)(2,1)} %constant.35.clone.back_t) | copy-start | bytes 248836
